TPU v7x, 128 devices: a whole 4x4x4 slice. The times are simulated.
128 devices in a mesh: cfg: 2 (over core), seq: 64 (over z, y, x).
Axes of the slice: x: 4, y: 4, z: 4, core: 2. Of those that a mesh axis runs over, the one named last changes fastest.
Arguments:
- queries: bfloat16 [2, 49152, 2560], P('cfg', 'seq'), may hold values from -48 to 48
- keys: bfloat16 [2, 49152, 2560], P('cfg', 'seq'), may hold values from -11 to 11
- values: bfloat16 [2, 49152, 2560], P('cfg', 'seq'), may hold values from -6 to 6
- tile_lists: int32 [2, 768, 16], P('cfg', 'seq'), may hold values from -1 to 767, as said below
- tile_order: int32 [768], replicated, may hold values from 0 to 767, as said below
Outputs:
- guided: float32 [49152, 2560], P('seq', 'cfg')
Inputs may be any that keep to these rules, and one draw needn't show every extreme that they name: `tile_lists`: entry 0 of each list is the query tile itself; entries -1 are empty and come last; the named tiles of one list are distinct. For each pass, the tiles named by the lists of the query tiles on one index d of seq lie on indices d - 2 to d + 2, and at most 4 of them on any one index other than d; in every draw some index names exactly 4 tiles of a neighbour. `tile_order`: A permutation of the video tiles.
All inputs are finite; a program needn't handle non-finite values.
Results may differ from a plain program's by a relative error of at most 0.0022.
Values may be sent and summed in bfloat16 or wider, within the bound.
No kernel may reach another device: no remote copies, remote signals or barrier semaphores. Data moves between devices by JAX's collectives and lax.ppermute only.
A program may use at most 192 MiB of HBM per device.

v0:
```python
import jax
import jax.numpy as jnp
from jax import lax
from jax.sharding import PartitionSpec as P

HD = 128
RADIUS = 2


guidance_scale = 5.0


def shifted(value, axis, steps):
    count = lax.axis_size(axis)
    initial, last = (max(0, -steps), min(count, count - steps))
    return lax.ppermute(value, axis, [(source, source + steps) for source in range(initial, last)])


def swapped(shard, axis, bit):
    return lax.ppermute(shard, axis, [(i, i ^ 1 << bit) for i in range(lax.axis_size(axis))])


def attend_tile(item, pool_keys, pool_values, tile, head_count):
    query_tile, picks, present = item
    count = picks.shape[0]
    chosen_keys = pool_keys[:, picks].reshape(head_count, count * tile, HD)
    chosen_values = pool_values[:, picks].reshape(head_count, count * tile, HD)
    scores = jnp.einsum(
        "hqd,hkd->hqk", query_tile, chosen_keys, preferred_element_type=jnp.float32
    ) * HD ** (-0.5)
    allowed = jnp.repeat(present, tile)[None, None, :]
    scores = jnp.where(allowed, scores, -1e30)
    largest = jnp.max(scores, axis=-1, keepdims=True)
    weights = jnp.where(allowed, jnp.exp(scores - largest), 0.0)
    totals = jnp.sum(weights, axis=-1)
    mixed = jnp.einsum(
        "hqk,hkd->hqd",
        weights.astype(jnp.bfloat16),
        chosen_values,
        preferred_element_type=jnp.float32,
    )
    return mixed / totals[:, :, None]


def per_device(queries, keys, values, tile_lists, tile_order):
    query_rows = queries[0]
    key_rows = keys[0]
    value_rows = values[0]
    listed = tile_lists[0]
    tiles_here = listed.shape[0]
    rows, width = query_rows.shape
    tile = rows // tiles_here
    head_count = width // HD
    position = lax.axis_index("seq")
    all_tiles = tile_order.shape[0]
    matching = listed[:, :, None] == tile_order[None, None, :]
    slot_index = jnp.sum(jnp.where(matching, jnp.arange(all_tiles, dtype=jnp.int32), 0), axis=2)
    present = listed >= 0
    owner = slot_index // tiles_here
    local = slot_index % tiles_here
    distance_to = jnp.where(present, owner - position, 0)
    key_tiles = jnp.transpose(key_rows.reshape(tiles_here, tile, head_count, HD), (2, 0, 1, 3))
    value_tiles = jnp.transpose(value_rows.reshape(tiles_here, tile, head_count, HD), (2, 0, 1, 3))
    gathered_keys = [key_tiles]
    gathered_values = [value_tiles]
    pool_index = local
    filled = tiles_here
    reaches = list(range(-RADIUS, 0)) + list(range(1, RADIUS + 1))
    for distance in reaches:
        aimed = distance_to == distance
        arrived = shifted((key_tiles, value_tiles), "seq", -distance)
        pool_index = jnp.where(aimed, filled + local, pool_index)
        filled = filled + tiles_here
        gathered_keys.append(arrived[0])
        gathered_values.append(arrived[1])
    pool_keys = jnp.concatenate(gathered_keys, axis=1)
    pool_values = jnp.concatenate(gathered_values, axis=1)
    query_tiles = jnp.transpose(query_rows.reshape(tiles_here, tile, head_count, HD), (0, 2, 1, 3))
    attended = lax.map(
        lambda item: attend_tile(item, pool_keys, pool_values, tile, head_count),
        (query_tiles, pool_index, present),
    )
    attended = jnp.transpose(attended, (0, 2, 1, 3)).reshape(rows, width)
    half_width = width // 2
    side = lax.axis_index("cfg")
    kept = lax.dynamic_slice_in_dim(attended, side * half_width, half_width, 1)
    handed = lax.dynamic_slice_in_dim(attended, (1 - side) * half_width, half_width, 1)
    partner = swapped(handed, "cfg", 0)
    conditional = jnp.where(side == 0, kept, partner)
    unconditional = jnp.where(side == 0, partner, kept)
    return unconditional + guidance_scale * (conditional - unconditional)


def solution(mesh):
    return jax.shard_map(
        per_device,
        mesh=mesh,
        in_specs=(
            P("cfg", "seq", None),
            P("cfg", "seq", None),
            P("cfg", "seq", None),
            P("cfg", "seq", None),
            P(),
        ),
        out_specs=P("seq", "cfg"),
        check_vma=False,
    )
```

profile of v0, /device:TPU:64, one launch (start us, length us, event | category | flops | bytes accessed | tf_op | source)
XLA Modules:
  0.0 1075.9 jit_solution(13315736044911569354)
XLA Ops:
  48.6 58.9 %collective-permute-done.4 = bf16[20,12,64,128]{3,2,1,0:T(8,128)(2,1)} collective-permute-done((bf16[20,12,64,128]{3,2,1,0:T(8,128)(2,1)}, bf16[20,12,64,128]{3,2,1,0:T(8,128)(2,1)}, u32[]{:S(2)}, u32[]{:S(2)}) %collective-permute-start.4) | collective-permute-done | bytes 3932192 | tf_op jit(solution)/shard_map/ppermute | solution.py:16
  111.0 80.9 %collective-permute-done.5 = bf16[20,12,64,128]{3,2,1,0:T(8,128)(2,1)} collective-permute-done((bf16[20,12,64,128]{3,2,1,0:T(8,128)(2,1)}, bf16[20,12,64,128]{3,2,1,0:T(8,128)(2,1)}, u32[]{:S(2)}, u32[]{:S(2)}) %collective-permute-start.5) | collective-permute-done | bytes 3932192 | tf_op jit(solution)/shard_map/ppermute | solution.py:16
  239.8 34.4 %collective-permute-done.7 = bf16[20,12,64,128]{3,2,1,0:T(8,128)(2,1)} collective-permute-done((bf16[20,12,64,128]{3,2,1,0:T(8,128)(2,1)}, bf16[20,12,64,128]{3,2,1,0:T(8,128)(2,1)}, u32[]{:S(2)}, u32[]{:S(2)}) %collective-permute-start.7) | collective-permute-done | bytes 3932192 | tf_op jit(solution)/shard_map/ppermute | solution.py:16
  281.9 18.8 %copy.59 = bf16[20,60,64,128]{3,2,1,0:T(8,128)(2,1)} copy(bf16[20,60,64,128]{3,0,2,1:T(8,128)(2,1)} %copy_dynamic-update-slice_fusion) | data formatting | bytes 39321600 | tf_op jit(solution)/shard_map/while | solution.py:79
  300.7 59.7 %collective-permute-done = bf16[20,12,64,128]{3,2,1,0:T(8,128)(2,1)} collective-permute-done((bf16[20,12,64,128]{3,2,1,0:T(8,128)(2,1)}, bf16[20,12,64,128]{3,2,1,0:T(8,128)(2,1)}, u32[]{:S(2)}, u32[]{:S(2)}) %collective-permute-start) | collective-permute-done | bytes 3932192 | tf_op jit(solution)/shard_map/ppermute | solution.py:16
  365.9 78.6 %collective-permute-done.1 = bf16[20,12,64,128]{3,2,1,0:T(8,128)(2,1)} collective-permute-done((bf16[20,12,64,128]{3,2,1,0:T(8,128)(2,1)}, bf16[20,12,64,128]{3,2,1,0:T(8,128)(2,1)}, u32[]{:S(2)}, u32[]{:S(2)}) %collective-permute-start.1) | collective-permute-done | bytes 3932192 | tf_op jit(solution)/shard_map/ppermute | solution.py:16
  455.4 70.4 %collective-permute-done.3 = bf16[20,12,64,128]{3,2,1,0:T(8,128)(2,1)} collective-permute-done((bf16[20,12,64,128]{3,2,1,0:T(8,128)(2,1)}, bf16[20,12,64,128]{3,2,1,0:T(8,128)(2,1)}, u32[]{:S(2)}, u32[]{:S(2)}) %collective-permute-start.3) | collective-permute-done | bytes 3932192 | tf_op jit(solution)/shard_map/ppermute | solution.py:16
  540.3 506.8 %while.10 = (s32[]{:T(128)}, f32[12,20,64,128]{3,2,1,0:T(8,128)}, pred[12,16]{1,0:T(8,128)(4,1)S(1)}, bf16[12,20,64,128]{3,2,1,0:T(8,128)(2,1)}, s32[12,16]{1,0:...) while((s32[]{:T(128)}, f32[12,20,64,128]{3,2,1,0:T(8,128)}, ...), condition=%wide.region_4.5_spmd, body=%wide.region_1.4_spmd.sunk | while | flops 681740352 | bytes 69160392 | solution.py:79
  540.3 10.1 gather_fusion.1
  566.1 10.1 gather_fusion
  582.5 10.1 gather_fusion.1
  624.8 10.1 gather_fusion.1
  667.0 10.1 gather_fusion.1
  709.2 10.1 gather_fusion.1
  751.4 10.1 gather_fusion.1
  793.6 10.1 gather_fusion.1
  835.8 10.1 gather_fusion.1
  878.0 10.1 gather_fusion.1
  903.8 10.1 gather_fusion
  920.2 10.1 gather_fusion.1
  946.1 10.1 gather_fusion
  962.4 10.1 gather_fusion.1
  1004.7 10.1 gather_fusion.1
  1030.5 10.1 gather_fusion
  (176 shorter events, 511.9 us)
Async XLA Ops:
  13.0 94.6 %collective-permute-start.4 = (bf16[20,12,64,128]{3,2,1,0:T(8,128)(2,1)}, bf16[20,12,64,128]{3,2,1,0:T(8,128)(2,1)}, u32[]{:S(2)}, u32[]{:S(2)}) collective-permute-start(bf16[20,12,64,128]{3,2,1,0:T(8,128)(2,1)} %copy.49), channel_id=1, source_target_pairs={{0,2},{1,3},{2,4},{3,5},{4,6},{5,7},{6,8},{7,9},{8,10},{9,11},{10,... | collective-permute-start | bytes 11796488 | tf_op jit(solution)/shard_map/ppermute | solution.py:16
  17.9 174.0 %collective-permute-start.5 = (bf16[20,12,64,128]{3,2,1,0:T(8,128)(2,1)}, bf16[20,12,64,128]{3,2,1,0:T(8,128)(2,1)}, u32[]{:S(2)}, u32[]{:S(2)}) collective-permute-start(bf16[20,12,64,128]{3,2,1,0:T(8,128)(2,1)} %copy.49), channel_id=1, source_target_pairs={{0,1},{1,2},{2,3},{3,4},{4,5},{5,6},{6,7},{7,8},{8,9},{9,10},{10,1... | collective-permute-start | bytes 11796488 | tf_op jit(solution)/shard_map/ppermute | solution.py:16
  20.4 176.9 %collective-permute-start.6 = (bf16[20,12,64,128]{3,2,1,0:T(8,128)(2,1)}, bf16[20,12,64,128]{3,2,1,0:T(8,128)(2,1)}, u32[]{:S(2)}, u32[]{:S(2)}) collective-permute-start(bf16[20,12,64,128]{3,2,1,0:T(8,128)(2,1)} %copy.49), channel_id=1, source_target_pairs={{1,0},{2,1},{3,2},{4,3},{5,4},{6,5},{7,6},{8,7},{9,8},{10,9},{11,1... | collective-permute-start | bytes 11796488 | tf_op jit(solution)/shard_map/ppermute | solution.py:16
  28.0 246.2 %collective-permute-start.7 = (bf16[20,12,64,128]{3,2,1,0:T(8,128)(2,1)}, bf16[20,12,64,128]{3,2,1,0:T(8,128)(2,1)}, u32[]{:S(2)}, u32[]{:S(2)}) collective-permute-start(bf16[20,12,64,128]{3,2,1,0:T(8,128)(2,1)} %copy.49), channel_id=1, source_target_pairs={{2,0},{3,1},{4,2},{5,3},{6,4},{7,5},{8,6},{9,7},{10,8},{11,9},{12,... | collective-permute-start | bytes 11796488 | tf_op jit(solution)/shard_map/ppermute | solution.py:16
  37.5 73.4 %copy-start.1 = (s32[1,12,16]{2,0,1:T(1,128)S(1)}, s32[1,12,16]{2,0,1:T(1,128)}, u32[]{:S(2)}) copy-start(s32[1,12,16]{2,0,1:T(1,128)} %param.10) | copy-start | bytes 2308
  37.5 156.8 %slice-start = ((s8[4718592]{0:T(1024)(128)(4,1)}), s8[4194304]{0:T(1024)(128)(4,1)S(1)}, s32[]{:S(2)}) async-start(s8[4718592]{0:T(1024)(128)(4,1)} %bitcast.71), calls=%async_computation | async-start | bytes 8388608
  37.5 156.8 %slice-start.1 = ((s8[4718592]{0:T(1024)(128)(4,1)}), s8[524288]{0:T(1024)(128)(4,1)S(1)}, s32[]{:S(2)}) async-start(s8[4718592]{0:T(1024)(128)(4,1)} %bitcast.71), calls=%async_computation.1 | async-start | bytes 1048576
  43.1 158.1 %copy-start.2 = (s32[768]{0:T(1024)S(1)}, s32[768]{0:T(1024)}, u32[]{:S(2)}) copy-start(s32[768]{0:T(1024)} %param.11) | copy-start | bytes 9220
  43.1 317.3 %collective-permute-start = (bf16[20,12,64,128]{3,2,1,0:T(8,128)(2,1)}, bf16[20,12,64,128]{3,2,1,0:T(8,128)(2,1)}, u32[]{:S(2)}, u32[]{:S(2)}) collective-permute-start(bf16[20,12,64,128]{3,2,1,0:T(8,128)(2,1)} %copy.41), channel_id=1, source_target_pairs={{0,2},{1,3},{2,4},{3,5},{4,6},{5,7},{6,8},{7,9},{8,10},{9,11},{10,... | collective-permute-start | bytes 11796488 | tf_op jit(solution)/shard_map/ppermute | solution.py:16
  107.6 336.9 %collective-permute-start.1 = (bf16[20,12,64,128]{3,2,1,0:T(8,128)(2,1)}, bf16[20,12,64,128]{3,2,1,0:T(8,128)(2,1)}, u32[]{:S(2)}, u32[]{:S(2)}) collective-permute-start(bf16[20,12,64,128]{3,2,1,0:T(8,128)(2,1)} %copy.41), channel_id=1, source_target_pairs={{0,1},{1,2},{2,3},{3,4},{4,5},{5,6},{6,7},{7,8},{8,9},{9,10},{10,1... | collective-permute-start | bytes 11796488 | tf_op jit(solution)/shard_map/ppermute | solution.py:16
  191.9 258.1 %collective-permute-start.2 = (bf16[20,12,64,128]{3,2,1,0:T(8,128)(2,1)}, bf16[20,12,64,128]{3,2,1,0:T(8,128)(2,1)}, u32[]{:S(2)}, u32[]{:S(2)}) collective-permute-start(bf16[20,12,64,128]{3,2,1,0:T(8,128)(2,1)} %copy.41), channel_id=1, source_target_pairs={{1,0},{2,1},{3,2},{4,3},{5,4},{6,5},{7,6},{8,7},{9,8},{10,9},{11,1... | collective-permute-start | bytes 11796488 | tf_op jit(solution)/shard_map/ppermute | solution.py:16
  197.3 328.5 %collective-permute-start.3 = (bf16[20,12,64,128]{3,2,1,0:T(8,128)(2,1)}, bf16[20,12,64,128]{3,2,1,0:T(8,128)(2,1)}, u32[]{:S(2)}, u32[]{:S(2)}) collective-permute-start(bf16[20,12,64,128]{3,2,1,0:T(8,128)(2,1)} %copy.41), channel_id=1, source_target_pairs={{2,0},{3,1},{4,2},{5,3},{6,4},{7,5},{8,6},{9,7},{10,8},{11,9},{12,... | collective-permute-start | bytes 11796488 | tf_op jit(solution)/shard_map/ppermute | solution.py:16
  1057.4 3.1 copy-start
  1062.7 7.1 collective-permute-start.8
where the time goes:
time: 1080 us
  local copies, waits for them, and re-layouts  487 us (45%)
  waiting for transfers between devices  390 us (36%)
  matrix products  86.3 us (8%)
  other arithmetic  79.9 us (7%)
  starting transfers between devices  32.2 us (3%)
    ppermute x8, waiting for transfers between devices, shifted(): lax.ppermute(value, axis, [(source, source + steps) for source in range(i...  383 us
    gather x24, local copies, waits for them, and re-layouts, attend_tile(): chosen_keys = pool_keys[:, picks].reshape(head_count, count * tile, HD)  172 us
    gather x24, local copies, waits for them, and re-layouts, attend_tile(): chosen_values = pool_values[:, picks].reshape(head_count, count * tile, HD)  172 us
    sub x12, other arithmetic, attend_tile(): weights = jnp.where(allowed, jnp.exp(scores - largest), 0.0)  73.4 us
    dot_general x12, matrix products, attend_tile(): jnp.einsum('hqd,hkd->hqk', query_tile, chosen_keys, preferred_element_typ...  62.2 us
    unnamed x20, local copies, waits for them, and re-layouts  49.3 us
    while x3, local copies, waits for them, and re-layouts, per_device(): lax.map(lambda item: attend_tile(item, pool_keys, pool_values, tile, head...  33.1 us
    ppermute x8, starting transfers between devices, shifted(): lax.ppermute(value, axis, [(source, source + steps) for source in range(i...  32.2 us
  transfers between devices with their start and end apart: 9, of which 7 were waited for; matrix products, arithmetic and copies ran while one was open for 9% of the time, Pallas kernels for 0%

commit v1 on v0

v1 whole, which is shorter than its diff:
```python
import functools

import jax
import jax.numpy as jnp
from jax import lax
from jax.experimental import pallas as pl
from jax.experimental.pallas import tpu as pltpu
from jax.sharding import PartitionSpec as P

HD = 128
CAP = 4
GROUP = 4
REACHES = (1, -1, 2, -2)
HANDED = ((0, 6), (6, 4))
KEPT = ((0, 6), (6, 4))
guidance_scale = 5.0
ANY = pl.BlockSpec(memory_space=pl.ANY)
SMEM = pl.BlockSpec(memory_space=pltpu.SMEM)
VMEM = pl.BlockSpec(memory_space=pltpu.VMEM)
SHORT = pl.CostEstimate(flops=1, bytes_accessed=1, transcendentals=0)
PARAMS = pltpu.CompilerParams(vmem_limit_bytes=63 * 1024 * 1024)


def shifted(value, axis, steps):
    count = lax.axis_size(axis)
    initial, last = (max(0, -steps), min(count, count - steps))
    return lax.ppermute(value, axis, [(source, source + steps) for source in range(initial, last)])


def any_equal(listed, tile_id):
    return jnp.max((listed == tile_id).astype(jnp.int32))


def pack(tile, start, picks, keys, values, outs, pools, load_sems, sems, plan=None, wait=True):
    width = pools.shape[2]
    columns = pl.ds(pl.multiple_of(start, HD), width)
    loads = [
        pltpu.make_async_copy(source.at[:, columns], pools.at[kind], load_sems.at[kind])
        for kind, source in enumerate((keys, values))
    ]
    for copy in loads:
        copy.start()
    if plan is not None:
        plan()
    copies = []
    for kind in range(2):
        loads[kind].wait()
        for reach in range(len(outs)):
            for entry in range(CAP):
                first = pl.multiple_of(picks[reach, entry] * tile, tile)
                copy = pltpu.make_async_copy(
                    pools.at[kind, pl.ds(first, tile), :],
                    outs[reach].at[kind, pl.ds(entry * tile, tile), :],
                    sems.at[len(copies)],
                )
                copy.start()
                copies.append(copy)
    if wait:
        for copy in copies:
            copy.wait()
    return copies


def first_pack_kernel(tile, tiles_here, place, order, *refs):
    listed = refs[:2]
    keys, values = refs[2:4]
    outs = refs[-7:-5]
    picks_out, picks, pools, load_sems, sems = refs[-5:]
    base = place[0] * tiles_here

    def plan():
        for reach in range(2):
            wanted = listed[reach][...]
            filled = jnp.int32(0)
            for entry in range(CAP):
                picks[reach, entry] = 0
            for slot in range(tiles_here):
                picks[reach, filled] = slot
                filled = jnp.minimum(filled + any_equal(wanted, order[base + slot]), CAP)
            for entry in range(CAP):
                picks_out[reach, entry] = picks[reach, entry]

    pack(tile, place[1], picks, keys, values, outs, pools, load_sems, sems, plan)


def later_pack_kernel(tile, count, place, near, far, keys, values, *refs):
    class Picks:
        def __getitem__(self, at):
            return (near if at[0] < 2 else far)[at[0] % 2, at[1]]

    outs, scratch = refs[-(len(REACHES) + 3) * count : -3 * count], refs[-3 * count :]
    waits = []
    for chunk in range(count):
        mine = outs[len(REACHES) * chunk : len(REACHES) * (chunk + 1)]
        waits += pack(tile, place[chunk], Picks(), keys, values, mine, *scratch[3 * chunk : 3 * chunk + 3], wait=False)
    for copy in waits:
        copy.wait()


def index_kernel(tiles_here, devices, place, order, listed_ref, index_ref):
    listed = listed_ref[...]
    here = place[0]
    index = jnp.zeros_like(listed)
    for slot in range(tiles_here):
        index = jnp.where(listed == order[here * tiles_here + slot], slot, index)
    for reach, distance in enumerate(REACHES):
        there = here + distance
        inside = jnp.logical_and(there >= 0, there < devices)
        base = jnp.where(inside, there, here) * tiles_here
        filled = jnp.int32(0)
        for slot in range(tiles_here):
            tile_id = jnp.where(inside, order[base + slot], -2)
            index = jnp.where(listed == tile_id, tiles_here + CAP * reach + filled, index)
            filled = jnp.minimum(filled + any_equal(listed, tile_id), CAP - 1)
    index_ref[...] = index


def attend_kernel(heads, tile, tiles_here, topk, kept, place, index, counts, queries, keys, values, *refs):
    arrived = refs[: len(REACHES)]
    rest = refs[len(REACHES) :]
    out, q_pool, k_pool, v_pool, scores, tops, result, other_pool, in_sems, out_sems = rest[-10:]
    width = heads * HD
    rows = tile * tiles_here
    columns = pl.ds(pl.multiple_of(place[1], HD), width)
    copies = [pltpu.make_async_copy(queries.at[:, columns], q_pool, in_sems.at[0])]
    for kind, (own, pool) in enumerate(((keys, k_pool), (values, v_pool))):
        copies.append(pltpu.make_async_copy(own.at[:, columns], pool.at[pl.ds(0, rows), :], in_sems.at[len(copies)]))
        for reach in range(len(REACHES)):
            copies.append(
                pltpu.make_async_copy(
                    arrived[reach].at[kind],
                    pool.at[pl.ds(rows + reach * CAP * tile, CAP * tile), :],
                    in_sems.at[len(copies)],
                )
            )
    before_scores = 2 + len(REACHES)
    if kept is not None:
        for piece, (to, source, count) in enumerate(kept[1:]):
            copies.append(
                pltpu.make_async_copy(
                    rest[piece].at[:, pl.ds(source, count)],
                    other_pool.at[:, pl.ds(to, count)],
                    in_sems.at[len(copies)],
                )
            )
        out = out.at[:, pl.ds(kept[0], width)]
    for copy in copies:
        copy.start()
    factor = HD ** (-0.5) * 1.4426950408889634
    side = place[0]
    span = GROUP * tile
    groups = topk // GROUP
    zeros = jnp.zeros((tile, HD), jnp.bfloat16)

    def rows_of(i):
        return pl.ds(pl.multiple_of(i * tile, tile), tile)

    def gathered(pool, i, group, pair):
        picks = [pl.multiple_of(index[i, group * GROUP + j] * tile, tile) for j in range(GROUP)]
        return jnp.concatenate([pool[pl.ds(p, tile), pair * 2 * HD : (pair + 1) * 2 * HD] for p in picks], axis=0)

    def score(i, slot):
        for pair in range(heads // 2):
            lanes = [slice((2 * pair + j) * HD, (2 * pair + j + 1) * HD) for j in range(2)]
            query = jnp.concatenate(
                [
                    jnp.concatenate([q_pool[rows_of(i), lanes[0]], zeros], axis=1),
                    jnp.concatenate([zeros, q_pool[rows_of(i), lanes[1]]], axis=1),
                ],
                axis=0,
            )
            top = jnp.full((2 * tile, HD), -jnp.inf, jnp.float32)
            for group in range(groups):
                part = lax.dot_general(
                    query,
                    gathered(k_pool, i, group, pair),
                    (((1,), (1,)), ((), ())),
                    preferred_element_type=jnp.float32,
                )
                place_of = lax.broadcasted_iota(jnp.int32, (1, span), 1) + group * span
                part = jnp.where(place_of < counts[i] * tile, part, -1e30)
                scores[slot, pair, :, group * span : (group + 1) * span] = part
                for j in range(span // HD):
                    top = jnp.maximum(top, part[:, j * HD : (j + 1) * HD])
            tops[slot, pair] = jnp.broadcast_to(jnp.max(top, axis=1, keepdims=True), top.shape)

    def mix(i, slot):
        for pair in range(heads // 2):
            top = tops[slot, pair]
            total = jnp.zeros((2 * tile, HD), jnp.float32)
            mixed = [jnp.zeros((tile, HD), jnp.float32)] * 2
            for group in range(groups):
                rounded = []
                for j in range(span // HD):
                    first = group * span + j * HD
                    weights = jnp.exp2((scores[slot, pair, :, first : first + HD] - top) * factor)
                    total = total + weights
                    rounded.append(weights.astype(jnp.bfloat16))
                both = jnp.dot(
                    jnp.concatenate(rounded, axis=1),
                    gathered(v_pool, i, group, pair),
                    preferred_element_type=jnp.float32,
                )
                mixed = [mixed[0] + both[:tile, :HD], mixed[1] + both[tile:, HD:]]
            total = jnp.sum(total, axis=1, keepdims=True)
            for j in range(2):
                lanes = slice((2 * pair + j) * HD, (2 * pair + j + 1) * HD)
                attended = mixed[j] / total[j * tile : (j + 1) * tile]
                if kept is not None:
                    other = other_pool[rows_of(i), lanes]
                    conditional = jnp.where(side == 0, attended, other)
                    unconditional = jnp.where(side == 0, other, attended)
                    attended = unconditional + guidance_scale * (conditional - unconditional)
                result[rows_of(i), lanes] = attended

    def copy_out(step):
        here = pl.ds(pl.multiple_of(step * 2 * tile, 2 * tile), 2 * tile)
        return pltpu.make_async_copy(result.at[here, :], out.at[here, :], out_sems.at[step])

    for copy in copies[:before_scores]:
        copy.wait()
    score(0, 0)
    for copy in copies[before_scores:]:
        copy.wait()

    def two_tiles(step, carry):
        i = step * 2
        score(i + 1, 1)
        mix(i, 0)
        score(jnp.minimum(i + 2, tiles_here - 1), 0)
        mix(i + 1, 1)
        copy_out(step).start()
        return carry

    lax.fori_loop(0, tiles_here // 2, two_tiles, 0)
    for step in range(tiles_here // 2):
        copy_out(step).wait()


def per_device(queries, keys, values, tile_lists, tile_order):
    queries, keys, values, listed = queries[0], keys[0], values[0], tile_lists[0]
    tiles_here, topk = listed.shape
    rows, features = queries.shape
    tile = rows // tiles_here
    devices = lax.axis_size("seq")
    side, position = lax.axis_index("cfg"), lax.axis_index("seq")
    half = features // 2
    neighbours = len(REACHES)
    chunks = []
    for kept, parts, first in ((False, HANDED, (1 - side) * half), (True, KEPT, side * half)):
        for head, heads in parts:
            chunks.append((kept, head, heads, (first + head * HD).astype(jnp.int32)))

    asked = [shifted(listed, "seq", distance) for distance in REACHES]

    def buffers(chunk, count):
        width = chunks[chunk][2] * HD
        return [jax.ShapeDtypeStruct((2, CAP * tile, width), keys.dtype)] * count

    def pools(chunk, count):
        width = chunks[chunk][2] * HD
        return [
            pltpu.VMEM((2, rows, width), keys.dtype),
            pltpu.SemaphoreType.DMA((2,)),
            pltpu.SemaphoreType.DMA((2 * count * CAP,)),
        ]

    def first_pack(lists, after):
        table = jax.ShapeDtypeStruct((2, CAP + 4), jnp.int32)
        return pl.pallas_call(
            functools.partial(first_pack_kernel, tile, tiles_here),
            out_shape=buffers(0, 2) + [table],
            in_specs=[SMEM, SMEM, VMEM, VMEM] + [ANY] * (2 + len(after)),
            out_specs=[ANY, ANY, SMEM],
            scratch_shapes=[pltpu.SMEM(table.shape, jnp.int32)] + pools(0, 2),
            compiler_params=PARAMS,
            cost_estimate=SHORT,
            name="first_pack",
        )(jnp.stack([position, chunks[0][3]]).astype(jnp.int32), tile_order, *lists, keys, values, *after)

    def later_pack(picks, after):
        later = range(1, len(chunks))
        made = pl.pallas_call(
            functools.partial(later_pack_kernel, tile, len(later)),
            out_shape=sum([buffers(chunk, neighbours) for chunk in later], []),
            in_specs=[SMEM, SMEM, SMEM, ANY, ANY] + [ANY] * len(after),
            out_specs=[ANY] * (neighbours * len(later)),
            scratch_shapes=sum([pools(chunk, neighbours) for chunk in later], []),
            compiler_params=PARAMS,
            cost_estimate=SHORT,
            name="later_pack",
        )(jnp.stack([chunks[chunk][3] for chunk in later]), *picks, keys, values, *after)
        return [list(made[i : i + neighbours]) for i in range(0, len(made), neighbours)]

    def moved(sending):
        return [shifted(buffer, "seq", -distance) for buffer, distance in zip(sending, REACHES)]

    index = pl.pallas_call(
        functools.partial(index_kernel, tiles_here, devices),
        out_shape=jax.ShapeDtypeStruct(listed.shape, jnp.int32),
        in_specs=[SMEM, SMEM, VMEM],
        out_specs=VMEM,
        compiler_params=PARAMS,
        cost_estimate=SHORT,
        name="pool_index",
    )(position.astype(jnp.int32)[None], tile_order, listed)
    counts = jnp.sum((listed >= 0).astype(jnp.int32), axis=1)

    *near, near_picks = first_pack(asked[:2], [])
    *far, far_picks = first_pack(asked[2:], near[:1])
    arrived = [moved(near + far)]
    arrived += [moved(sending) for sending in later_pack([near_picks, far_picks], [arrived[0][2], index])]
    partners, guided, result = [], None, None
    pool = tiles_here * tile + neighbours * CAP * tile
    for chunk, (kept, head, heads, start) in enumerate(chunks):
        width = heads * HD
        operands = [jnp.stack([side, start]).astype(jnp.int32), index, counts, queries, keys, values]
        operands += arrived[chunk]
        aliases, columns = {}, None
        if kept:
            columns = [head * HD]
            for handed_head, handed_heads, partner in partners:
                first, last = max(head, handed_head), min(head + heads, handed_head + handed_heads)
                if first < last:
                    operands.append(partner)
                    columns.append(((first - head) * HD, (first - handed_head) * HD, (last - first) * HD))
        if guided is None and result is not None:
            operands.append(result)
        if guided is not None:
            aliases = {len(operands): 0}
            operands.append(guided)
        out_shape = jax.ShapeDtypeStruct((rows, half if kept else width), jnp.float32)
        result = pl.pallas_call(
            functools.partial(attend_kernel, heads, tile, tiles_here, topk, columns),
            out_shape=out_shape,
            in_specs=[SMEM] * 3 + [ANY] * (len(operands) - 3),
            out_specs=ANY,
            input_output_aliases=aliases,
            scratch_shapes=[
                pltpu.VMEM((rows, width), jnp.bfloat16),
                pltpu.VMEM((pool, width), jnp.bfloat16),
                pltpu.VMEM((pool, width), jnp.bfloat16),
                pltpu.VMEM((2, heads // 2, 2 * tile, topk * tile), jnp.float32),
                pltpu.VMEM((2, heads // 2, 2 * tile, HD), jnp.float32),
                pltpu.VMEM((rows, width), jnp.float32),
                pltpu.VMEM((rows, width) if kept else (8, HD), jnp.float32),
                pltpu.SemaphoreType.DMA((16,)),
                pltpu.SemaphoreType.DMA((tiles_here // 2,)),
            ],
            compiler_params=PARAMS,
            cost_estimate=pl.CostEstimate(
                flops=10000 * rows * topk * tile * width,
                bytes_accessed=100000 * rows * width,
                transcendentals=rows * topk * tile * heads,
            ),
            name=("guide_" if kept else "attend_") + str(chunk),
        )(*operands)
        if kept:
            guided = result
        else:
            partners.append((head, heads, lax.ppermute(result, "cfg", [(0, 1), (1, 0)])))
    return guided


def solution(mesh):
    return jax.shard_map(
        per_device,
        mesh=mesh,
        in_specs=(
            P("cfg", "seq", None),
            P("cfg", "seq", None),
            P("cfg", "seq", None),
            P("cfg", "seq", None),
            P(),
        ),
        out_specs=P("seq", "cfg"),
        check_vma=False,
    )
```

time: 1080 us -> 227 us (0.21)
  local copies, waits for them, and re-layouts: 487 us -> 2.77 us
  waiting for transfers between devices: 390 us -> 68.1 us
  matrix products: 86.3 us -> 0 us
  other arithmetic: 79.9 us -> 3.79 us
  Pallas kernels: 0 us -> 73.2 us
  starting transfers between devices: 32.2 us -> 77.6 us
    gather x48 -> x0, local copies, waits for them, and re-layouts: 344 us -> none  [the longest x24 172 us: attend_tile(): chosen_keys = pool_keys[:, picks].reshape(head_count, count * tile, HD)]
    ppermute x8 -> x20, waiting for transfers between devices: 383 us -> 68.1 us  [shifted(): lax.ppermute(value, axis, [(source, source + steps) for source in range(i...]
    dot_general x24 -> x0, matrix products: 86.3 us -> none  [the longest x12 62.2 us: attend_tile(): jnp.einsum('hqd,hkd->hqk', query_tile, chosen_keys, preferred_element_typ...]
    sub x12 -> x0, other arithmetic: 73.4 us -> none  [attend_tile(): weights = jnp.where(allowed, jnp.exp(scores - largest), 0.0)]
    pallas_call x0 -> x8, Pallas kernels: none -> 73.2 us  [the longest x4 54.8 us: per_device(): pl.pallas_call(functools.partial(attend_kernel, heads, tile, tiles_here,...]
    unnamed x20 -> x15, local copies, waits for them, and re-layouts: 49.3 us -> 2.77 us
    ppermute x8 -> x20, starting transfers between devices: 32.2 us -> 77.4 us  [shifted(): lax.ppermute(value, axis, [(source, source + steps) for source in range(i...]
    while x3 -> x0, local copies, waits for them, and re-layouts: 33.1 us -> none  [per_device(): lax.map(lambda item: attend_tile(item, pool_keys, pool_values, tile, head...]
  transfers between devices with their start and end apart: 9 -> 22, of which waited for: 7 -> 6; matrix products, arithmetic and copies ran while one was open for 9% -> 2% of each run, Pallas kernels for 0% -> 25%
where the time goes in v1:
time: 227 us; the launch traced here: 226 us
  starting transfers between devices  77.6 us (34%)
  Pallas kernels  73.2 us (32%)
  waiting for transfers between devices  68.1 us (30%)
  other arithmetic  3.79 us (2%)
  local copies, waits for them, and re-layouts  2.77 us (1%)
    ppermute x20, starting transfers between devices, shifted(): lax.ppermute(value, axis, [(source, source + steps) for source in range(i...  77.4 us
    ppermute x20, waiting for transfers between devices, shifted(): lax.ppermute(value, axis, [(source, source + steps) for source in range(i...  68.1 us
    pallas_call x4, Pallas kernels, per_device(): pl.pallas_call(functools.partial(attend_kernel, heads, tile, tiles_here,...  54.8 us
    pallas_call x2, Pallas kernels, first_pack(): pl.pallas_call(functools.partial(first_pack_kernel, tile, tiles_here), ou...  8.54 us
    pallas_call x1, Pallas kernels, later_pack(): pl.pallas_call(functools.partial(later_pack_kernel, tile, len(later)), ou...  8.24 us
  transfers between devices with their start and end apart: 22, of which 6 were waited for; matrix products, arithmetic and copies ran while one was open for 2% of the time, Pallas kernels for 25%

profile of v1, /device:TPU:64, one launch (start us, length us, event | category | flops | bytes accessed | tf_op | source)
XLA Modules:
  0.0 225.8 jit_solution(1457745238946053064)
XLA Ops:
  0.7 3.4 %collective-permute-start = (s32[12,16]{1,0:T(8,128)S(1)}, s32[12,16]{1,0:T(8,128)S(1)}, u32[]{:S(2)}, u32[]{:S(2)}) collective-permute-start(s32[12,16]{1,0:T(8,128)S(1)} %bitcast.28), channel_id=1, source_target_pairs={{0,1},{1,2},{2,3},{3,4},{4,5},{5,6},{6,7},{7,8},{8,9},{9,10},{10,1... | collective-permute-start | bytes 2312 | tf_op jit(solution)/shard_map/ppermute | solution.py:27
  4.1 6.7 %collective-permute-start.1 = (s32[12,16]{1,0:T(8,128)S(1)}, s32[12,16]{1,0:T(8,128)S(1)}, u32[]{:S(2)}, u32[]{:S(2)}) collective-permute-start(s32[12,16]{1,0:T(8,128)S(1)} %bitcast.29), channel_id=1, source_target_pairs={{1,0},{2,1},{3,2},{4,3},{5,4},{6,5},{7,6},{8,7},{9,8},{10,9},{11,1... | collective-permute-start | bytes 2312 | tf_op jit(solution)/shard_map/ppermute | solution.py:27
  12.7 8.4 %collective-permute-start.3 = (s32[12,16]{1,0:T(8,128)S(1)}, s32[12,16]{1,0:T(8,128)S(1)}, u32[]{:S(2)}, u32[]{:S(2)}) collective-permute-start(s32[12,16]{1,0:T(8,128)S(1)} %bitcast.31), channel_id=1, source_target_pairs={{2,0},{3,1},{4,2},{5,3},{6,4},{7,5},{8,6},{9,7},{10,8},{11,9},{12,... | collective-permute-start | bytes 2312 | tf_op jit(solution)/shard_map/ppermute | solution.py:27
  22.4 4.2 %first_pack.2 = (bf16[2,256,768]{2,1,0:T(8,128)(2,1)}, bf16[2,256,768]{2,1,0:T(8,128)(2,1)}, s32[2,8]{1,0:T(2,128)}) custom-call(s32[2]{0:T(128)} %pad_add_fusion.2.place, s32[768]{0:T(1024)} %order.5, s32[12,16]{1,0:T(8,128)} %copy-done.3, s32[12,16]{1,0:T(8,128)} %copy-done.4, bf16[768,2560]{1,0:T(8,128)(2,1)} %bitcast.14, bf16[768,2560]{1,0:T(8,128)(2,1)} %bitcast.21), custom_call_target="tpu_custom_call" | custom-call | flops 1 | bytes 1 | tf_op jit(solution)/shard_map/first_pack/pallas_call | solution.py:270
  27.2 4.4 %first_pack.3 = (bf16[2,256,768]{2,1,0:T(8,128)(2,1)}, bf16[2,256,768]{2,1,0:T(8,128)(2,1)}, s32[2,8]{1,0:T(2,128)}) custom-call(s32[2]{0:T(128)} %pad_add_fusion.2.place, s32[768]{0:T(1024)} %order.5, s32[12,16]{1,0:T(8,128)} %copy-done.5, s32[12,16]{1,0:T(8,128)} %copy-done.6, bf16[768,2560]{1,0:T(8,128)(2,1)} %bitcast.15, bf16[768,2560]{1,0:T(8,128)(2,1)} %bitcast.22, ...), custom_call_target="tpu_custom_call" | custom-call | flops 1 | bytes 1 | tf_op jit(solution)/shard_map/first_pack/pallas_call | solution.py:270
  31.6 4.6 %collective-permute-start.4 = (bf16[2,256,768]{2,1,0:T(8,128)(2,1)}, bf16[2,256,768]{2,1,0:T(8,128)(2,1)S(1)}, u32[]{:S(2)}, u32[]{:S(2)}) collective-permute-start(bf16[2,256,768]{2,1,0:T(8,128)(2,1)} %get-tuple-element.26), channel_id=1, source_target_pairs={{2,0},{3,1},{4,2},{5,3},{6,4},{7,5},{8,6},{9,7},{10,8},{11,9},{12,... | collective-permute-start | bytes 2359304 | tf_op jit(solution)/shard_map/ppermute | solution.py:27
  36.2 2.8 %collective-permute-start.15 = (bf16[2,256,768]{2,1,0:T(8,128)(2,1)}, bf16[2,256,768]{2,1,0:T(8,128)(2,1)}, u32[]{:S(2)}, u32[]{:S(2)}) collective-permute-start(bf16[2,256,768]{2,1,0:T(8,128)(2,1)} %get-tuple-element.36), channel_id=1, source_target_pairs={{0,2},{1,3},{2,4},{3,5},{4,6},{5,7},{6,8},{7,9},{8,10},{9,11},{10,... | collective-permute-start | bytes 2359304 | tf_op jit(solution)/shard_map/ppermute | solution.py:27
  38.9 4.0 %collective-permute-start.13 = (bf16[2,256,768]{2,1,0:T(8,128)(2,1)}, bf16[2,256,768]{2,1,0:T(8,128)(2,1)}, u32[]{:S(2)}, u32[]{:S(2)}) collective-permute-start(bf16[2,256,768]{2,1,0:T(8,128)(2,1)} %get-tuple-element.24.refs_4_), channel_id=1, source_target_pairs={{1,0},{2,1},{3,2},{4,3},{5,4},{6,5},{7,6},{8,7},{9,8},{10,9},{11,1... | collective-permute-start | bytes 2359304 | tf_op jit(solution)/shard_map/ppermute | solution.py:27
  49.7 6.1 %collective-permute-done.4.refs_0_.refs_2_ = bf16[2,256,768]{2,1,0:T(8,128)(2,1)S(1)} collective-permute-done((bf16[2,256,768]{2,1,0:T(8,128)(2,1)}, bf16[2,256,768]{2,1,0:T(8,128)(2,1)S(1)}, u32[]{:S(2)}, u32[]{:S(2)}) %collective-permute-start.4) | collective-permute-done | bytes 786464 | tf_op jit(solution)/shard_map/ppermute | solution.py:27
  56.6 8.2 %later_pack.1 = (bf16[2,256,512]{2,1,0:T(8,128)(2,1)}, bf16[2,256,512]{2,1,0:T(8,128)(2,1)}, bf16[2,256,512]{2,1,0:T(8,128)(2,1)}, bf16[2,256,512]{2,1,0:T(8,128...) custom-call(s32[3]{0:T(128)} %pad_add_fusion.1.place, ...), custom_call_target="tpu_custom_call" | custom-call | flops 1 | bytes 1 | tf_op jit(solution)/shard_map/later_pack/pallas_call | solution.py:283
  66.8 7.6 %collective-permute-start.11 = (bf16[2,256,512]{2,1,0:T(8,128)(2,1)}, bf16[2,256,512]{2,1,0:T(8,128)(2,1)}, u32[]{:S(2)}, u32[]{:S(2)}) collective-permute-start(bf16[2,256,512]{2,1,0:T(8,128)(2,1)} %get-tuple-element.33), channel_id=1, source_target_pairs={{2,0},{3,1},{4,2},{5,3},{6,4},{7,5},{8,6},{9,7},{10,8},{11,9},{12,... | collective-permute-start | bytes 1572872 | tf_op jit(solution)/shard_map/ppermute | solution.py:27
  74.4 2.8 %collective-permute-start.12 = (bf16[2,256,512]{2,1,0:T(8,128)(2,1)}, bf16[2,256,512]{2,1,0:T(8,128)(2,1)}, u32[]{:S(2)}, u32[]{:S(2)}) collective-permute-start(bf16[2,256,512]{2,1,0:T(8,128)(2,1)} %get-tuple-element.34), channel_id=1, source_target_pairs={{0,2},{1,3},{2,4},{3,5},{4,6},{5,7},{6,8},{7,9},{8,10},{9,11},{10,... | collective-permute-start | bytes 1572872 | tf_op jit(solution)/shard_map/ppermute | solution.py:27
  77.2 8.7 %collective-permute-done.13.refs_0_ = bf16[2,256,768]{2,1,0:T(8,128)(2,1)} collective-permute-done((bf16[2,256,768]{2,1,0:T(8,128)(2,1)}, bf16[2,256,768]{2,1,0:T(8,128)(2,1)}, u32[]{:S(2)}, u32[]{:S(2)}) %collective-permute-start.13) | collective-permute-done | bytes 786464 | tf_op jit(solution)/shard_map/ppermute | solution.py:27
  85.9 7.5 %collective-permute-start.9 = (bf16[2,256,512]{2,1,0:T(8,128)(2,1)}, bf16[2,256,512]{2,1,0:T(8,128)(2,1)}, u32[]{:S(2)}, u32[]{:S(2)}) collective-permute-start(bf16[2,256,512]{2,1,0:T(8,128)(2,1)} %get-tuple-element.31), channel_id=1, source_target_pairs={{1,0},{2,1},{3,2},{4,3},{5,4},{6,5},{7,6},{8,7},{9,8},{10,9},{11,1... | collective-permute-start | bytes 1572872 | tf_op jit(solution)/shard_map/ppermute | solution.py:27
  93.4 15.3 %attend_0.1.refs_4_ = f32[768,768]{1,0:T(8,128)} custom-call(s32[2]{0:T(128)} %pad_add_fusion.5.place, s32[12,16]{1,0:T(8,128)} %pool_index.1.refs_1_.index, s32[12]{0:T(128)} %convert_reduce_fusion.counts, bf16[768,2560]{1,0:T(8,128)(2,1)} %bitcast.33, bf16[768,2560]{1,0:T(8,128)(2,1)} %bitcast.17, bf16[768,2560]{1,0:T(8,128)(2,1)} %bitcast.24, ...), custom_call_target="tpu_custom_call" | custom-call | flops 6039797760000 | bytes 58982400000 | tf_op jit(solution)/shard_map/attend_0/pallas_call | solution.py:333
  114.7 7.6 %collective-permute-done.12.refs_3_ = bf16[2,256,512]{2,1,0:T(8,128)(2,1)} collective-permute-done((bf16[2,256,512]{2,1,0:T(8,128)(2,1)}, bf16[2,256,512]{2,1,0:T(8,128)(2,1)}, u32[]{:S(2)}, u32[]{:S(2)}) %collective-permute-start.12) | collective-permute-done | bytes 524320 | tf_op jit(solution)/shard_map/ppermute | solution.py:27
  124.3 5.4 %collective-permute-start.20 = (bf16[2,256,768]{2,1,0:T(8,128)(2,1)}, bf16[2,256,768]{2,1,0:T(8,128)(2,1)}, u32[]{:S(2)}, u32[]{:S(2)}) collective-permute-start(bf16[2,256,768]{2,1,0:T(8,128)(2,1)} %get-tuple-element.40), channel_id=1, source_target_pairs={{0,2},{1,3},{2,4},{3,5},{4,6},{5,7},{6,8},{7,9},{8,10},{9,11},{10,... | collective-permute-start | bytes 2359304 | tf_op jit(solution)/shard_map/ppermute | solution.py:27
  129.7 11.3 %attend_1.1.refs_5_ = f32[768,512]{1,0:T(8,128)} custom-call(s32[2]{0:T(128)} %pad_add_fusion.3.place, s32[12,16]{1,0:T(8,128)} %pool_index.1.refs_1_.index, s32[12]{0:T(128)} %convert_reduce_fusion.counts, bf16[768,2560]{1,0:T(8,128)(2,1)} %bitcast.34, bf16[768,2560]{1,0:T(8,128)(2,1)} %bitcast.18, bf16[768,2560]{1,0:T(8,128)(2,1)} %bitcast.25, ...), custom_call_target="tpu_custom_call" | custom-call | flops 4026531840000 | bytes 39321600000 | tf_op jit(solution)/shard_map/attend_1/pallas_call | solution.py:333
  143.8 28.1 %collective-permute-done.18.refs_1_ = bf16[2,256,768]{2,1,0:T(8,128)(2,1)} collective-permute-done((bf16[2,256,768]{2,1,0:T(8,128)(2,1)}, bf16[2,256,768]{2,1,0:T(8,128)(2,1)}, u32[]{:S(2)}, u32[]{:S(2)}) %collective-permute-start.18) | collective-permute-done | bytes 786464 | tf_op jit(solution)/shard_map/ppermute | solution.py:27
  173.8 2.9 %collective-permute-start.7 = (bf16[2,256,512]{2,1,0:T(8,128)(2,1)}, bf16[2,256,512]{2,1,0:T(8,128)(2,1)}, u32[]{:S(2)}, u32[]{:S(2)}) collective-permute-start(bf16[2,256,512]{2,1,0:T(8,128)(2,1)} %get-tuple-element.29), channel_id=1, source_target_pairs={{2,0},{3,1},{4,2},{5,3},{6,4},{7,5},{8,6},{9,7},{10,8},{11,9},{12,... | collective-permute-start | bytes 1572872 | tf_op jit(solution)/shard_map/ppermute | solution.py:27
  176.7 4.4 %collective-permute-start.8 = (bf16[2,256,512]{2,1,0:T(8,128)(2,1)}, bf16[2,256,512]{2,1,0:T(8,128)(2,1)}, u32[]{:S(2)}, u32[]{:S(2)}) collective-permute-start(bf16[2,256,512]{2,1,0:T(8,128)(2,1)} %get-tuple-element.30), channel_id=1, source_target_pairs={{0,2},{1,3},{2,4},{3,5},{4,6},{5,7},{6,8},{7,9},{8,10},{9,11},{10,... | collective-permute-start | bytes 1572872 | tf_op jit(solution)/shard_map/ppermute | solution.py:27
  181.3 16.2 %guide_2.1.refs_5_ = f32[768,1280]{1,0:T(8,128)} custom-call(s32[2]{0:T(128)} %get-tuple-element.42.place, s32[12,16]{1,0:T(8,128)} %pool_index.1.refs_1_.index, s32[12]{0:T(128)} %convert_reduce_fusion.counts, bf16[768,2560]{1,0:T(8,128)(2,1)} %bitcast.35, bf16[768,2560]{1,0:T(8,128)(2,1)} %bitcast.19, bf16[768,2560]{1,0:T(8,128)(2,1)} %bitcast.26, ...), custom_call_target="tpu_custom_call" | custom-call | flops 6039797760000 | bytes 58982400000 | tf_op jit(solution)/shard_map/guide_2/pallas_call | solution.py:333
  197.5 16.3 %collective-permute-done.6.refs_1_ = bf16[2,256,512]{2,1,0:T(8,128)(2,1)} collective-permute-done((bf16[2,256,512]{2,1,0:T(8,128)(2,1)}, bf16[2,256,512]{2,1,0:T(8,128)(2,1)}, u32[]{:S(2)}, u32[]{:S(2)}) %collective-permute-start.6) | collective-permute-done | bytes 524320 | tf_op jit(solution)/shard_map/ppermute | solution.py:27
  213.8 11.9 %guide_3.1 = f32[768,1280]{1,0:T(8,128)} custom-call(s32[2]{0:T(128)} %get-tuple-element.41.place, s32[12,16]{1,0:T(8,128)} %pool_index.1.refs_1_.index, s32[12]{0:T(128)} %convert_reduce_fusion.counts, bf16[768,2560]{1,0:T(8,128)(2,1)} %bitcast.36, bf16[768,2560]{1,0:T(8,128)(2,1)} %bitcast.20, ...), custom_call_target="tpu_custom_call", output_to_operand_aliasing={{}: (11, {})} | custom-call | flops 4026531840000 | bytes 39321600000 | tf_op jit(solution)/shard_map/guide_3/pallas_call | solution.py:333
  (49 shorter events, 26.5 us)
Async XLA Ops:
  0.7 25.9 %copy-start.1 = (s32[1,12,16]{2,1,0:T(8,128)}, s32[1,12,16]{2,1,0:T(8,128)S(1)}, u32[]{:S(2)}) copy-start(s32[1,12,16]{2,1,0:T(8,128)S(1)} %copy.11) | copy-start | bytes 2308
  0.7 21.1 %collective-permute-start = (s32[12,16]{1,0:T(8,128)S(1)}, s32[12,16]{1,0:T(8,128)S(1)}, u32[]{:S(2)}, u32[]{:S(2)}) collective-permute-start(s32[12,16]{1,0:T(8,128)S(1)} %bitcast.28), channel_id=1, source_target_pairs={{0,1},{1,2},{2,3},{3,4},{4,5},{5,6},{6,7},{7,8},{8,9},{9,10},{10,1... | collective-permute-start | bytes 2312 | tf_op jit(solution)/shard_map/ppermute | solution.py:27
  4.1 17.7 %collective-permute-start.1 = (s32[12,16]{1,0:T(8,128)S(1)}, s32[12,16]{1,0:T(8,128)S(1)}, u32[]{:S(2)}, u32[]{:S(2)}) collective-permute-start(s32[12,16]{1,0:T(8,128)S(1)} %bitcast.29), channel_id=1, source_target_pairs={{1,0},{2,1},{3,2},{4,3},{5,4},{6,5},{7,6},{8,7},{9,8},{10,9},{11,1... | collective-permute-start | bytes 2312 | tf_op jit(solution)/shard_map/ppermute | solution.py:27
  10.8 15.8 %collective-permute-start.2 = (s32[12,16]{1,0:T(8,128)S(1)}, s32[12,16]{1,0:T(8,128)S(1)}, u32[]{:S(2)}, u32[]{:S(2)}) collective-permute-start(s32[12,16]{1,0:T(8,128)S(1)} %bitcast.30), channel_id=1, source_target_pairs={{0,2},{1,3},{2,4},{3,5},{4,6},{5,7},{6,8},{7,9},{8,10},{9,11},{10,... | collective-permute-start | bytes 2312 | tf_op jit(solution)/shard_map/ppermute | solution.py:27
  12.7 13.9 %collective-permute-start.3 = (s32[12,16]{1,0:T(8,128)S(1)}, s32[12,16]{1,0:T(8,128)S(1)}, u32[]{:S(2)}, u32[]{:S(2)}) collective-permute-start(s32[12,16]{1,0:T(8,128)S(1)} %bitcast.31), channel_id=1, source_target_pairs={{2,0},{3,1},{4,2},{5,3},{6,4},{7,5},{8,6},{9,7},{10,8},{11,9},{12,... | collective-permute-start | bytes 2312 | tf_op jit(solution)/shard_map/ppermute | solution.py:27
  27.2 21.8 %copy-start.2 = (s32[1,12,16]{2,0,1:T(1,128)S(1)}, s32[1,12,16]{2,0,1:T(1,128)}, u32[]{:S(2)}) copy-start(s32[1,12,16]{2,0,1:T(1,128)} %param.8) | copy-start | bytes 2308
  31.6 24.2 %collective-permute-start.4 = (bf16[2,256,768]{2,1,0:T(8,128)(2,1)}, bf16[2,256,768]{2,1,0:T(8,128)(2,1)S(1)}, u32[]{:S(2)}, u32[]{:S(2)}) collective-permute-start(bf16[2,256,768]{2,1,0:T(8,128)(2,1)} %get-tuple-element.26), channel_id=1, source_target_pairs={{2,0},{3,1},{4,2},{5,3},{6,4},{7,5},{8,6},{9,7},{10,8},{11,9},{12,... | collective-permute-start | bytes 2359304 | tf_op jit(solution)/shard_map/ppermute | solution.py:27
  36.2 38.3 %collective-permute-start.15 = (bf16[2,256,768]{2,1,0:T(8,128)(2,1)}, bf16[2,256,768]{2,1,0:T(8,128)(2,1)}, u32[]{:S(2)}, u32[]{:S(2)}) collective-permute-start(bf16[2,256,768]{2,1,0:T(8,128)(2,1)} %get-tuple-element.36), channel_id=1, source_target_pairs={{0,2},{1,3},{2,4},{3,5},{4,6},{5,7},{6,8},{7,9},{8,10},{9,11},{10,... | collective-permute-start | bytes 2359304 | tf_op jit(solution)/shard_map/ppermute | solution.py:27
  38.9 47.0 %collective-permute-start.13 = (bf16[2,256,768]{2,1,0:T(8,128)(2,1)}, bf16[2,256,768]{2,1,0:T(8,128)(2,1)}, u32[]{:S(2)}, u32[]{:S(2)}) collective-permute-start(bf16[2,256,768]{2,1,0:T(8,128)(2,1)} %get-tuple-element.24.refs_4_), channel_id=1, source_target_pairs={{1,0},{2,1},{3,2},{4,3},{5,4},{6,5},{7,6},{8,7},{9,8},{10,9},{11,1... | collective-permute-start | bytes 2359304 | tf_op jit(solution)/shard_map/ppermute | solution.py:27
  42.9 50.5 %collective-permute-start.14 = (bf16[2,256,768]{2,1,0:T(8,128)(2,1)}, bf16[2,256,768]{2,1,0:T(8,128)(2,1)}, u32[]{:S(2)}, u32[]{:S(2)}) collective-permute-start(bf16[2,256,768]{2,1,0:T(8,128)(2,1)} %get-tuple-element.35), channel_id=1, source_target_pairs={{0,1},{1,2},{2,3},{3,4},{4,5},{5,6},{6,7},{7,8},{8,9},{9,10},{10,1... | collective-permute-start | bytes 2359304 | tf_op jit(solution)/shard_map/ppermute | solution.py:27
  64.9 43.9 %collective-permute-start.10 = (bf16[2,256,512]{2,1,0:T(8,128)(2,1)}, bf16[2,256,512]{2,1,0:T(8,128)(2,1)}, u32[]{:S(2)}, u32[]{:S(2)}) collective-permute-start(bf16[2,256,512]{2,1,0:T(8,128)(2,1)} %get-tuple-element.32), channel_id=1, source_target_pairs={{0,1},{1,2},{2,3},{3,4},{4,5},{5,6},{6,7},{7,8},{8,9},{9,10},{10,1... | collective-permute-start | bytes 1572872 | tf_op jit(solution)/shard_map/ppermute | solution.py:27
  66.8 45.2 %collective-permute-start.11 = (bf16[2,256,512]{2,1,0:T(8,128)(2,1)}, bf16[2,256,512]{2,1,0:T(8,128)(2,1)}, u32[]{:S(2)}, u32[]{:S(2)}) collective-permute-start(bf16[2,256,512]{2,1,0:T(8,128)(2,1)} %get-tuple-element.33), channel_id=1, source_target_pairs={{2,0},{3,1},{4,2},{5,3},{6,4},{7,5},{8,6},{9,7},{10,8},{11,9},{12,... | collective-permute-start | bytes 1572872 | tf_op jit(solution)/shard_map/ppermute | solution.py:27
  74.4 47.9 %collective-permute-start.12 = (bf16[2,256,512]{2,1,0:T(8,128)(2,1)}, bf16[2,256,512]{2,1,0:T(8,128)(2,1)}, u32[]{:S(2)}, u32[]{:S(2)}) collective-permute-start(bf16[2,256,512]{2,1,0:T(8,128)(2,1)} %get-tuple-element.34), channel_id=1, source_target_pairs={{0,2},{1,3},{2,4},{3,5},{4,6},{5,7},{6,8},{7,9},{8,10},{9,11},{10,... | collective-permute-start | bytes 1572872 | tf_op jit(solution)/shard_map/ppermute | solution.py:27
  85.9 38.4 %collective-permute-start.9 = (bf16[2,256,512]{2,1,0:T(8,128)(2,1)}, bf16[2,256,512]{2,1,0:T(8,128)(2,1)}, u32[]{:S(2)}, u32[]{:S(2)}) collective-permute-start(bf16[2,256,512]{2,1,0:T(8,128)(2,1)} %get-tuple-element.31), channel_id=1, source_target_pairs={{1,0},{2,1},{3,2},{4,3},{5,4},{6,5},{7,6},{8,7},{9,8},{10,9},{11,1... | collective-permute-start | bytes 1572872 | tf_op jit(solution)/shard_map/ppermute | solution.py:27
  108.7 72.5 %collective-permute-start.21 = (f32[768,768]{1,0:T(8,128)}, f32[768,768]{1,0:T(8,128)}, u32[]{:S(2)}, u32[]{:S(2)}) collective-permute-start(f32[768,768]{1,0:T(8,128)} %attend_0.1.refs_4_), channel_id=1, source_target_pairs={{0,64},{64,0},{1,65},{65,1},{2,66},{66,2},{3,67},{67,3},{4,68},{68... | collective-permute-start | bytes 7077896 | tf_op jit(solution)/shard_map/ppermute | solution.py:361
  108.9 32.2 %collective-permute-start.17 = (bf16[2,256,768]{2,1,0:T(8,128)(2,1)}, bf16[2,256,768]{2,1,0:T(8,128)(2,1)}, u32[]{:S(2)}, u32[]{:S(2)}) collective-permute-start(bf16[2,256,768]{2,1,0:T(8,128)(2,1)} %get-tuple-element.37), channel_id=1, source_target_pairs={{1,0},{2,1},{3,2},{4,3},{5,4},{6,5},{7,6},{8,7},{9,8},{10,9},{11,1... | collective-permute-start | bytes 2359304 | tf_op jit(solution)/shard_map/ppermute | solution.py:27
  112.0 59.9 %collective-permute-start.18 = (bf16[2,256,768]{2,1,0:T(8,128)(2,1)}, bf16[2,256,768]{2,1,0:T(8,128)(2,1)}, u32[]{:S(2)}, u32[]{:S(2)}) collective-permute-start(bf16[2,256,768]{2,1,0:T(8,128)(2,1)} %get-tuple-element.38), channel_id=1, source_target_pairs={{0,1},{1,2},{2,3},{3,4},{4,5},{5,6},{6,7},{7,8},{8,9},{9,10},{10,1... | collective-permute-start | bytes 2359304 | tf_op jit(solution)/shard_map/ppermute | solution.py:27
  122.4 51.4 %collective-permute-start.19 = (bf16[2,256,768]{2,1,0:T(8,128)(2,1)}, bf16[2,256,768]{2,1,0:T(8,128)(2,1)}, u32[]{:S(2)}, u32[]{:S(2)}) collective-permute-start(bf16[2,256,768]{2,1,0:T(8,128)(2,1)} %get-tuple-element.39), channel_id=1, source_target_pairs={{2,0},{3,1},{4,2},{5,3},{6,4},{7,5},{8,6},{9,7},{10,8},{11,9},{12,... | collective-permute-start | bytes 2359304 | tf_op jit(solution)/shard_map/ppermute | solution.py:27
  124.3 52.4 %collective-permute-start.20 = (bf16[2,256,768]{2,1,0:T(8,128)(2,1)}, bf16[2,256,768]{2,1,0:T(8,128)(2,1)}, u32[]{:S(2)}, u32[]{:S(2)}) collective-permute-start(bf16[2,256,768]{2,1,0:T(8,128)(2,1)} %get-tuple-element.40), channel_id=1, source_target_pairs={{0,2},{1,3},{2,4},{3,5},{4,6},{5,7},{6,8},{7,9},{8,10},{9,11},{10,... | collective-permute-start | bytes 2359304 | tf_op jit(solution)/shard_map/ppermute | solution.py:27
  141.1 56.5 %collective-permute-start.5 = (bf16[2,256,512]{2,1,0:T(8,128)(2,1)}, bf16[2,256,512]{2,1,0:T(8,128)(2,1)}, u32[]{:S(2)}, u32[]{:S(2)}) collective-permute-start(bf16[2,256,512]{2,1,0:T(8,128)(2,1)} %get-tuple-element.27), channel_id=1, source_target_pairs={{1,0},{2,1},{3,2},{4,3},{5,4},{6,5},{7,6},{8,7},{9,8},{10,9},{11,1... | collective-permute-start | bytes 1572872 | tf_op jit(solution)/shard_map/ppermute | solution.py:27
  171.9 41.9 %collective-permute-start.6 = (bf16[2,256,512]{2,1,0:T(8,128)(2,1)}, bf16[2,256,512]{2,1,0:T(8,128)(2,1)}, u32[]{:S(2)}, u32[]{:S(2)}) collective-permute-start(bf16[2,256,512]{2,1,0:T(8,128)(2,1)} %get-tuple-element.28), channel_id=1, source_target_pairs={{0,1},{1,2},{2,3},{3,4},{4,5},{5,6},{6,7},{7,8},{8,9},{9,10},{10,1... | collective-permute-start | bytes 1572872 | tf_op jit(solution)/shard_map/ppermute | solution.py:27
  173.8 40.0 %collective-permute-start.7 = (bf16[2,256,512]{2,1,0:T(8,128)(2,1)}, bf16[2,256,512]{2,1,0:T(8,128)(2,1)}, u32[]{:S(2)}, u32[]{:S(2)}) collective-permute-start(bf16[2,256,512]{2,1,0:T(8,128)(2,1)} %get-tuple-element.29), channel_id=1, source_target_pairs={{2,0},{3,1},{4,2},{5,3},{6,4},{7,5},{8,6},{9,7},{10,8},{11,9},{12,... | collective-permute-start | bytes 1572872 | tf_op jit(solution)/shard_map/ppermute | solution.py:27
  176.7 37.1 %collective-permute-start.8 = (bf16[2,256,512]{2,1,0:T(8,128)(2,1)}, bf16[2,256,512]{2,1,0:T(8,128)(2,1)}, u32[]{:S(2)}, u32[]{:S(2)}) collective-permute-start(bf16[2,256,512]{2,1,0:T(8,128)(2,1)} %get-tuple-element.30), channel_id=1, source_target_pairs={{0,2},{1,3},{2,4},{3,5},{4,6},{5,7},{6,8},{7,9},{8,10},{9,11},{10,... | collective-permute-start | bytes 1572872 | tf_op jit(solution)/shard_map/ppermute | solution.py:27
  181.2 32.6 %collective-permute-start.16 = (f32[768,512]{1,0:T(8,128)}, f32[768,512]{1,0:T(8,128)}, u32[]{:S(2)}, u32[]{:S(2)}) collective-permute-start(f32[768,512]{1,0:T(8,128)} %attend_1.1.refs_5_), channel_id=1, source_target_pairs={{0,64},{64,0},{1,65},{65,1},{2,66},{66,2},{3,67},{67,3},{4,68},{68... | collective-permute-start | bytes 4718600 | tf_op jit(solution)/shard_map/ppermute | solution.py:361
  (5 other events, 3.3 us)

commit v2 on v1

--- a/solution.py
+++ b/solution.py
@@ -17,6 +17,7 @@
 ANY = pl.BlockSpec(memory_space=pl.ANY)
 SMEM = pl.BlockSpec(memory_space=pltpu.SMEM)
 VMEM = pl.BlockSpec(memory_space=pltpu.VMEM)
+LONG = pl.CostEstimate(flops=10**13, bytes_accessed=10**11, transcendentals=0)
 SHORT = pl.CostEstimate(flops=1, bytes_accessed=1, transcendentals=0)
 PARAMS = pltpu.CompilerParams(vmem_limit_bytes=63 * 1024 * 1024)
 
@@ -62,37 +63,40 @@
 
 
 def first_pack_kernel(tile, tiles_here, place, order, *refs):
-    listed = refs[:2]
-    keys, values = refs[2:4]
-    outs = refs[-7:-5]
+    listed = refs[: len(REACHES)]
+    keys, values = refs[len(REACHES) : len(REACHES) + 2]
+    outs = refs[-5 - len(REACHES) : -5]
     picks_out, picks, pools, load_sems, sems = refs[-5:]
     base = place[0] * tiles_here
 
     def plan():
-        for reach in range(2):
+        for reach in range(len(REACHES)):
             wanted = listed[reach][...]
+            counts = []
+            for first in range(0, tiles_here, 6):
+                packed = jnp.zeros(wanted.shape, jnp.float32)
+                for slot in range(first, first + 6):
+                    packed = jnp.where(wanted == order[base + slot], float(16 ** (slot - first)), packed)
+                total = jnp.sum(packed).astype(jnp.int32)
+                counts += [(total >> (4 * j)) & 15 for j in range(6)]
             filled = jnp.int32(0)
             for entry in range(CAP):
                 picks[reach, entry] = 0
             for slot in range(tiles_here):
                 picks[reach, filled] = slot
-                filled = jnp.minimum(filled + any_equal(wanted, order[base + slot]), CAP)
+                filled = jnp.minimum(filled + jnp.minimum(counts[slot], 1), CAP)
             for entry in range(CAP):
                 picks_out[reach, entry] = picks[reach, entry]
 
     pack(tile, place[1], picks, keys, values, outs, pools, load_sems, sems, plan)
 
 
-def later_pack_kernel(tile, count, place, near, far, keys, values, *refs):
-    class Picks:
-        def __getitem__(self, at):
-            return (near if at[0] < 2 else far)[at[0] % 2, at[1]]
-
+def later_pack_kernel(tile, count, place, picks, keys, values, *refs):
     outs, scratch = refs[-(len(REACHES) + 3) * count : -3 * count], refs[-3 * count :]
     waits = []
     for chunk in range(count):
         mine = outs[len(REACHES) * chunk : len(REACHES) * (chunk + 1)]
-        waits += pack(tile, place[chunk], Picks(), keys, values, mine, *scratch[3 * chunk : 3 * chunk + 3], wait=False)
+        waits += pack(tile, place[chunk], picks, keys, values, mine, *scratch[3 * chunk : 3 * chunk + 3], wait=False)
     for copy in waits:
         copy.wait()
 
@@ -251,8 +255,6 @@
         for head, heads in parts:
             chunks.append((kept, head, heads, (first + head * HD).astype(jnp.int32)))
 
-    asked = [shifted(listed, "seq", distance) for distance in REACHES]
-
     def buffers(chunk, count):
         width = chunks[chunk][2] * HD
         return [jax.ShapeDtypeStruct((2, CAP * tile, width), keys.dtype)] * count
@@ -265,36 +267,40 @@
             pltpu.SemaphoreType.DMA((2 * count * CAP,)),
         ]
 
-    def first_pack(lists, after):
-        table = jax.ShapeDtypeStruct((2, CAP + 4), jnp.int32)
+    def first_pack(lists):
+        table = jax.ShapeDtypeStruct((neighbours, CAP + 4), jnp.int32)
         return pl.pallas_call(
             functools.partial(first_pack_kernel, tile, tiles_here),
-            out_shape=buffers(0, 2) + [table],
-            in_specs=[SMEM, SMEM, VMEM, VMEM] + [ANY] * (2 + len(after)),
-            out_specs=[ANY, ANY, SMEM],
-            scratch_shapes=[pltpu.SMEM(table.shape, jnp.int32)] + pools(0, 2),
+            out_shape=buffers(0, neighbours) + [table],
+            in_specs=[SMEM, SMEM] + [VMEM] * neighbours + [ANY, ANY],
+            out_specs=[ANY] * neighbours + [SMEM],
+            scratch_shapes=[pltpu.SMEM(table.shape, jnp.int32)] + pools(0, neighbours),
             compiler_params=PARAMS,
             cost_estimate=SHORT,
             name="first_pack",
-        )(jnp.stack([position, chunks[0][3]]).astype(jnp.int32), tile_order, *lists, keys, values, *after)
+        )(jnp.stack([position, chunks[0][3]]).astype(jnp.int32), tile_order, *lists, keys, values)
 
     def later_pack(picks, after):
         later = range(1, len(chunks))
         made = pl.pallas_call(
             functools.partial(later_pack_kernel, tile, len(later)),
             out_shape=sum([buffers(chunk, neighbours) for chunk in later], []),
-            in_specs=[SMEM, SMEM, SMEM, ANY, ANY] + [ANY] * len(after),
+            in_specs=[SMEM, SMEM, ANY, ANY] + [ANY] * len(after),
             out_specs=[ANY] * (neighbours * len(later)),
             scratch_shapes=sum([pools(chunk, neighbours) for chunk in later], []),
             compiler_params=PARAMS,
             cost_estimate=SHORT,
             name="later_pack",
-        )(jnp.stack([chunks[chunk][3] for chunk in later]), *picks, keys, values, *after)
+        )(jnp.stack([chunks[chunk][3] for chunk in later]), picks, keys, values, *after)
         return [list(made[i : i + neighbours]) for i in range(0, len(made), neighbours)]
 
     def moved(sending):
         return [shifted(buffer, "seq", -distance) for buffer, distance in zip(sending, REACHES)]
 
+    counts = jnp.sum((listed >= 0).astype(jnp.int32), axis=1)
+
+    asked = [shifted(listed, "seq", distance) for distance in REACHES]
+    *sending, picks = first_pack(asked)
     index = pl.pallas_call(
         functools.partial(index_kernel, tiles_here, devices),
         out_shape=jax.ShapeDtypeStruct(listed.shape, jnp.int32),
@@ -304,12 +310,8 @@
         cost_estimate=SHORT,
         name="pool_index",
     )(position.astype(jnp.int32)[None], tile_order, listed)
-    counts = jnp.sum((listed >= 0).astype(jnp.int32), axis=1)
-
-    *near, near_picks = first_pack(asked[:2], [])
-    *far, far_picks = first_pack(asked[2:], near[:1])
-    arrived = [moved(near + far)]
-    arrived += [moved(sending) for sending in later_pack([near_picks, far_picks], [arrived[0][2], index])]
+    arrived = [moved(sending)]
+    arrived += [moved(sending) for sending in later_pack(picks, [arrived[0][2], index])]
     partners, guided, result = [], None, None
     pool = tiles_here * tile + neighbours * CAP * tile
     for chunk, (kept, head, heads, start) in enumerate(chunks):
@@ -348,11 +350,7 @@
                 pltpu.SemaphoreType.DMA((tiles_here // 2,)),
             ],
             compiler_params=PARAMS,
-            cost_estimate=pl.CostEstimate(
-                flops=10000 * rows * topk * tile * width,
-                bytes_accessed=100000 * rows * width,
-                transcendentals=rows * topk * tile * heads,
-            ),
+            cost_estimate=LONG,
             name=("guide_" if kept else "attend_") + str(chunk),
         )(*operands)
         if kept:

time: 227 us -> 218 us (0.960)
  waiting for transfers between devices: 68.1 us -> 45.1 us
  starting transfers between devices: 77.6 us -> 95.5 us
  Pallas kernels: 73.2 us -> 69.6 us
    ppermute x20, waiting for transfers between devices: 68.1 us -> 45.1 us  [shifted(): lax.ppermute(value, axis, [(source, source + steps) for source in range(i...]
    ppermute x20, starting transfers between devices: 77.4 us -> 95.3 us  [shifted(): lax.ppermute(value, axis, [(source, source + steps) for source in range(i...]
    pallas_call x2 -> x1, Pallas kernels: 8.54 us -> 4.93 us  [first_pack(): pl.pallas_call(functools.partial(first_pack_kernel, tile, tiles_here), ou...]
  transfers between devices with their start and end apart: 22 -> 22, of which waited for: 6 -> 9; matrix products, arithmetic and copies ran while one was open for 2% -> 2% of each run, Pallas kernels for 25% -> 24%
where the time goes in v2:
time: 218 us; the launch traced here: 216 us
  starting transfers between devices  95.5 us (44%)
  Pallas kernels  69.6 us (32%)
  waiting for transfers between devices  45.1 us (21%)
  other arithmetic  3.66 us (2%)
  local copies, waits for them, and re-layouts  2.18 us (1%)
    ppermute x20, starting transfers between devices, shifted(): lax.ppermute(value, axis, [(source, source + steps) for source in range(i...  95.3 us
    pallas_call x4, Pallas kernels, per_device(): pl.pallas_call(functools.partial(attend_kernel, heads, tile, tiles_here,...  54.8 us
    ppermute x20, waiting for transfers between devices, shifted(): lax.ppermute(value, axis, [(source, source + steps) for source in range(i...  45.1 us
    pallas_call x1, Pallas kernels, later_pack(): pl.pallas_call(functools.partial(later_pack_kernel, tile, len(later)), ou...  8.24 us
    pallas_call x1, Pallas kernels, first_pack(): pl.pallas_call(functools.partial(first_pack_kernel, tile, tiles_here), ou...  4.93 us
  transfers between devices with their start and end apart: 22, of which 9 were waited for; matrix products, arithmetic and copies ran while one was open for 2% of the time, Pallas kernels for 24%

profile of v2, /device:TPU:64, one launch (start us, length us, event | category | flops | bytes accessed | tf_op | source)
XLA Modules:
  0.0 216.4 jit_solution(15511955298600772298)
XLA Ops:
  0.7 3.4 %collective-permute-start = (s32[12,16]{1,0:T(8,128)S(1)}, s32[12,16]{1,0:T(8,128)S(1)}, u32[]{:S(2)}, u32[]{:S(2)}) collective-permute-start(s32[12,16]{1,0:T(8,128)S(1)} %bitcast.26), channel_id=1, source_target_pairs={{0,1},{1,2},{2,3},{3,4},{4,5},{5,6},{6,7},{7,8},{8,9},{9,10},{10,1... | collective-permute-start | bytes 2312 | tf_op jit(solution)/shard_map/ppermute | solution.py:28
  4.1 6.7 %collective-permute-start.1 = (s32[12,16]{1,0:T(8,128)S(1)}, s32[12,16]{1,0:T(8,128)S(1)}, u32[]{:S(2)}, u32[]{:S(2)}) collective-permute-start(s32[12,16]{1,0:T(8,128)S(1)} %bitcast.27), channel_id=1, source_target_pairs={{1,0},{2,1},{3,2},{4,3},{5,4},{6,5},{7,6},{8,7},{9,8},{10,9},{11,1... | collective-permute-start | bytes 2312 | tf_op jit(solution)/shard_map/ppermute | solution.py:28
  12.7 8.4 %collective-permute-start.3 = (s32[12,16]{1,0:T(8,128)S(1)}, s32[12,16]{1,0:T(8,128)S(1)}, u32[]{:S(2)}, u32[]{:S(2)}) collective-permute-start(s32[12,16]{1,0:T(8,128)S(1)} %bitcast.29), channel_id=1, source_target_pairs={{2,0},{3,1},{4,2},{5,3},{6,4},{7,5},{8,6},{9,7},{10,8},{11,9},{12,... | collective-permute-start | bytes 2312 | tf_op jit(solution)/shard_map/ppermute | solution.py:28
  23.1 4.9 %first_pack.1 = (bf16[2,256,768]{2,1,0:T(8,128)(2,1)}, bf16[2,256,768]{2,1,0:T(8,128)(2,1)}, bf16[2,256,768]{2,1,0:T(8,128)(2,1)}, bf16[2,256,768]{2,1,0:T(8,128)(2,1)}, s32[4,8]{1,0:T(4,128)}) custom-call(s32[2]{0:T(128)} %pad_add_fusion.2.place, s32[768]{0:T(1024)} %order.3, s32[12,16]{1,0:T(8,128)} %copy-done.3, s32[12,16]{1,0:T(8,128)} %copy-done.4, ...), custom_call_target="tpu_custom_call" | custom-call | flops 1 | bytes 1 | tf_op jit(solution)/shard_map/first_pack/pallas_call | solution.py:272
  28.0 8.7 %collective-permute-start.4 = (bf16[2,256,768]{2,1,0:T(8,128)(2,1)}, bf16[2,256,768]{2,1,0:T(8,128)(2,1)S(1)}, u32[]{:S(2)}, u32[]{:S(2)}) collective-permute-start(bf16[2,256,768]{2,1,0:T(8,128)(2,1)} %get-tuple-element.23), channel_id=1, source_target_pairs={{2,0},{3,1},{4,2},{5,3},{6,4},{7,5},{8,6},{9,7},{10,8},{11,9},{12,... | collective-permute-start | bytes 2359304 | tf_op jit(solution)/shard_map/ppermute | solution.py:28
  38.7 3.9 %collective-permute-start.14 = (bf16[2,256,768]{2,1,0:T(8,128)(2,1)}, bf16[2,256,768]{2,1,0:T(8,128)(2,1)}, u32[]{:S(2)}, u32[]{:S(2)}) collective-permute-start(bf16[2,256,768]{2,1,0:T(8,128)(2,1)} %get-tuple-element.33), channel_id=1, source_target_pairs={{0,1},{1,2},{2,3},{3,4},{4,5},{5,6},{6,7},{7,8},{8,9},{9,10},{10,1... | collective-permute-start | bytes 2359304 | tf_op jit(solution)/shard_map/ppermute | solution.py:28
  49.2 5.9 %collective-permute-done.4.refs_0_.refs_2_ = bf16[2,256,768]{2,1,0:T(8,128)(2,1)S(1)} collective-permute-done((bf16[2,256,768]{2,1,0:T(8,128)(2,1)}, bf16[2,256,768]{2,1,0:T(8,128)(2,1)S(1)}, u32[]{:S(2)}, u32[]{:S(2)}) %collective-permute-start.4) | collective-permute-done | bytes 786464 | tf_op jit(solution)/shard_map/ppermute | solution.py:28
  56.0 8.2 %later_pack.1 = (bf16[2,256,512]{2,1,0:T(8,128)(2,1)}, bf16[2,256,512]{2,1,0:T(8,128)(2,1)}, bf16[2,256,512]{2,1,0:T(8,128)(2,1)}, bf16[2,256,512]{2,1,0:T(8,128...) custom-call(s32[3]{0:T(128)} %pad_add_fusion.1.place, ...), custom_call_target="tpu_custom_call" | custom-call | flops 1 | bytes 1 | tf_op jit(solution)/shard_map/later_pack/pallas_call | solution.py:285
  66.1 8.8 %collective-permute-start.11 = (bf16[2,256,512]{2,1,0:T(8,128)(2,1)}, bf16[2,256,512]{2,1,0:T(8,128)(2,1)}, u32[]{:S(2)}, u32[]{:S(2)}) collective-permute-start(bf16[2,256,512]{2,1,0:T(8,128)(2,1)} %get-tuple-element.30), channel_id=1, source_target_pairs={{2,0},{3,1},{4,2},{5,3},{6,4},{7,5},{8,6},{9,7},{10,8},{11,9},{12,... | collective-permute-start | bytes 1572872 | tf_op jit(solution)/shard_map/ppermute | solution.py:28
  76.9 7.8 %collective-permute-start.9 = (bf16[2,256,512]{2,1,0:T(8,128)(2,1)}, bf16[2,256,512]{2,1,0:T(8,128)(2,1)}, u32[]{:S(2)}, u32[]{:S(2)}) collective-permute-start(bf16[2,256,512]{2,1,0:T(8,128)(2,1)} %get-tuple-element.28), channel_id=1, source_target_pairs={{1,0},{2,1},{3,2},{4,3},{5,4},{6,5},{7,6},{8,7},{9,8},{10,9},{11,1... | collective-permute-start | bytes 1572872 | tf_op jit(solution)/shard_map/ppermute | solution.py:28
  84.7 4.6 %collective-permute-done.15.refs_3_ = bf16[2,256,768]{2,1,0:T(8,128)(2,1)} collective-permute-done((bf16[2,256,768]{2,1,0:T(8,128)(2,1)}, bf16[2,256,768]{2,1,0:T(8,128)(2,1)}, u32[]{:S(2)}, u32[]{:S(2)}) %collective-permute-start.15) | collective-permute-done | bytes 786464 | tf_op jit(solution)/shard_map/ppermute | solution.py:28
  89.3 15.3 %attend_0.1.refs_4_ = f32[768,768]{1,0:T(8,128)} custom-call(s32[2]{0:T(128)} %pad_add_fusion.5.place, s32[12,16]{1,0:T(8,128)} %pool_index.1.refs_1_.index, s32[12]{0:T(128)} %convert_reduce_fusion.counts, bf16[768,2560]{1,0:T(8,128)(2,1)} %bitcast.31, bf16[768,2560]{1,0:T(8,128)(2,1)} %bitcast.16, bf16[768,2560]{1,0:T(8,128)(2,1)} %bitcast.22, ...), custom_call_target="tpu_custom_call" | custom-call | flops 9999999827968 | bytes 99999997952 | tf_op jit(solution)/shard_map/attend_0/pallas_call | solution.py:335
  106.6 4.7 %collective-permute-done.11.refs_2_ = bf16[2,256,512]{2,1,0:T(8,128)(2,1)} collective-permute-done((bf16[2,256,512]{2,1,0:T(8,128)(2,1)}, bf16[2,256,512]{2,1,0:T(8,128)(2,1)}, u32[]{:S(2)}, u32[]{:S(2)}) %collective-permute-start.11) | collective-permute-done | bytes 524320 | tf_op jit(solution)/shard_map/ppermute | solution.py:28
  113.2 9.8 %collective-permute-done.12.refs_3_ = bf16[2,256,512]{2,1,0:T(8,128)(2,1)} collective-permute-done((bf16[2,256,512]{2,1,0:T(8,128)(2,1)}, bf16[2,256,512]{2,1,0:T(8,128)(2,1)}, u32[]{:S(2)}, u32[]{:S(2)}) %collective-permute-start.12) | collective-permute-done | bytes 524320 | tf_op jit(solution)/shard_map/ppermute | solution.py:28
  124.9 5.5 %collective-permute-start.20 = (bf16[2,256,768]{2,1,0:T(8,128)(2,1)}, bf16[2,256,768]{2,1,0:T(8,128)(2,1)}, u32[]{:S(2)}, u32[]{:S(2)}) collective-permute-start(bf16[2,256,768]{2,1,0:T(8,128)(2,1)} %get-tuple-element.38), channel_id=1, source_target_pairs={{0,2},{1,3},{2,4},{3,5},{4,6},{5,7},{6,8},{7,9},{8,10},{9,11},{10,... | collective-permute-start | bytes 2359304 | tf_op jit(solution)/shard_map/ppermute | solution.py:28
  130.4 11.3 %attend_1.1.refs_5_ = f32[768,512]{1,0:T(8,128)} custom-call(s32[2]{0:T(128)} %pad_add_fusion.3.place, s32[12,16]{1,0:T(8,128)} %pool_index.1.refs_1_.index, s32[12]{0:T(128)} %convert_reduce_fusion.counts, bf16[768,2560]{1,0:T(8,128)(2,1)} %bitcast.32, bf16[768,2560]{1,0:T(8,128)(2,1)} %bitcast.17, bf16[768,2560]{1,0:T(8,128)(2,1)} %bitcast.23, ...), custom_call_target="tpu_custom_call" | custom-call | flops 9999999827968 | bytes 99999997952 | tf_op jit(solution)/shard_map/attend_1/pallas_call | solution.py:335
  141.7 2.9 %collective-permute-start.5 = (bf16[2,256,512]{2,1,0:T(8,128)(2,1)}, bf16[2,256,512]{2,1,0:T(8,128)(2,1)}, u32[]{:S(2)}, u32[]{:S(2)}) collective-permute-start(bf16[2,256,512]{2,1,0:T(8,128)(2,1)} %get-tuple-element.24), channel_id=1, source_target_pairs={{1,0},{2,1},{3,2},{4,3},{5,4},{6,5},{7,6},{8,7},{9,8},{10,9},{11,1... | collective-permute-start | bytes 1572872 | tf_op jit(solution)/shard_map/ppermute | solution.py:28
  144.6 3.0 %collective-permute-start.6 = (bf16[2,256,512]{2,1,0:T(8,128)(2,1)}, bf16[2,256,512]{2,1,0:T(8,128)(2,1)}, u32[]{:S(2)}, u32[]{:S(2)}) collective-permute-start(bf16[2,256,512]{2,1,0:T(8,128)(2,1)} %get-tuple-element.25), channel_id=1, source_target_pairs={{0,1},{1,2},{2,3},{3,4},{4,5},{5,6},{6,7},{7,8},{8,9},{9,10},{10,1... | collective-permute-start | bytes 1572872 | tf_op jit(solution)/shard_map/ppermute | solution.py:28
  147.6 8.7 %collective-permute-done.19.refs_2_ = bf16[2,256,768]{2,1,0:T(8,128)(2,1)} collective-permute-done((bf16[2,256,768]{2,1,0:T(8,128)(2,1)}, bf16[2,256,768]{2,1,0:T(8,128)(2,1)}, u32[]{:S(2)}, u32[]{:S(2)}) %collective-permute-start.19) | collective-permute-done | bytes 786464 | tf_op jit(solution)/shard_map/ppermute | solution.py:28
  156.3 15.5 %collective-permute-start.7 = (bf16[2,256,512]{2,1,0:T(8,128)(2,1)}, bf16[2,256,512]{2,1,0:T(8,128)(2,1)}, u32[]{:S(2)}, u32[]{:S(2)}) collective-permute-start(bf16[2,256,512]{2,1,0:T(8,128)(2,1)} %get-tuple-element.26), channel_id=1, source_target_pairs={{2,0},{3,1},{4,2},{5,3},{6,4},{7,5},{8,6},{9,7},{10,8},{11,9},{12,... | collective-permute-start | bytes 1572872 | tf_op jit(solution)/shard_map/ppermute | solution.py:28
  173.6 5.5 %collective-permute-start.8 = (bf16[2,256,512]{2,1,0:T(8,128)(2,1)}, bf16[2,256,512]{2,1,0:T(8,128)(2,1)}, u32[]{:S(2)}, u32[]{:S(2)}) collective-permute-start(bf16[2,256,512]{2,1,0:T(8,128)(2,1)} %get-tuple-element.27), channel_id=1, source_target_pairs={{0,2},{1,3},{2,4},{3,5},{4,6},{5,7},{6,8},{7,9},{8,10},{9,11},{10,... | collective-permute-start | bytes 1572872 | tf_op jit(solution)/shard_map/ppermute | solution.py:28
  179.2 16.2 %guide_2.1.refs_5_ = f32[768,1280]{1,0:T(8,128)} custom-call(s32[2]{0:T(128)} %get-tuple-element.40.place, s32[12,16]{1,0:T(8,128)} %pool_index.1.refs_1_.index, s32[12]{0:T(128)} %convert_reduce_fusion.counts, bf16[768,2560]{1,0:T(8,128)(2,1)} %bitcast.33, bf16[768,2560]{1,0:T(8,128)(2,1)} %bitcast.18, bf16[768,2560]{1,0:T(8,128)(2,1)} %bitcast.24, ...), custom_call_target="tpu_custom_call" | custom-call | flops 9999999827968 | bytes 99999997952 | tf_op jit(solution)/shard_map/guide_2/pallas_call | solution.py:335
  195.6 8.8 %collective-permute-done.8.refs_3_ = bf16[2,256,512]{2,1,0:T(8,128)(2,1)} collective-permute-done((bf16[2,256,512]{2,1,0:T(8,128)(2,1)}, bf16[2,256,512]{2,1,0:T(8,128)(2,1)}, u32[]{:S(2)}, u32[]{:S(2)}) %collective-permute-start.8) | collective-permute-done | bytes 524320 | tf_op jit(solution)/shard_map/ppermute | solution.py:28
  204.4 12.0 %guide_3.1 = f32[768,1280]{1,0:T(8,128)} custom-call(s32[2]{0:T(128)} %get-tuple-element.39.place, s32[12,16]{1,0:T(8,128)} %pool_index.1.refs_1_.index, s32[12]{0:T(128)} %convert_reduce_fusion.counts, bf16[768,2560]{1,0:T(8,128)(2,1)} %bitcast.34, bf16[768,2560]{1,0:T(8,128)(2,1)} %bitcast.19, ...), custom_call_target="tpu_custom_call", output_to_operand_aliasing={{}: (11, {})} | custom-call | flops 9999999827968 | bytes 99999997952 | tf_op jit(solution)/shard_map/guide_3/pallas_call | solution.py:335
  (48 shorter events, 25.7 us)
Async XLA Ops:
  0.7 27.3 %copy-start.1 = (s32[1,12,16]{2,1,0:T(8,128)}, s32[1,12,16]{2,1,0:T(8,128)S(1)}, u32[]{:S(2)}) copy-start(s32[1,12,16]{2,1,0:T(8,128)S(1)} %copy.11) | copy-start | bytes 2308
  0.7 21.0 %collective-permute-start = (s32[12,16]{1,0:T(8,128)S(1)}, s32[12,16]{1,0:T(8,128)S(1)}, u32[]{:S(2)}, u32[]{:S(2)}) collective-permute-start(s32[12,16]{1,0:T(8,128)S(1)} %bitcast.26), channel_id=1, source_target_pairs={{0,1},{1,2},{2,3},{3,4},{4,5},{5,6},{6,7},{7,8},{8,9},{9,10},{10,1... | collective-permute-start | bytes 2312 | tf_op jit(solution)/shard_map/ppermute | solution.py:28
  4.1 17.7 %collective-permute-start.1 = (s32[12,16]{1,0:T(8,128)S(1)}, s32[12,16]{1,0:T(8,128)S(1)}, u32[]{:S(2)}, u32[]{:S(2)}) collective-permute-start(s32[12,16]{1,0:T(8,128)S(1)} %bitcast.27), channel_id=1, source_target_pairs={{1,0},{2,1},{3,2},{4,3},{5,4},{6,5},{7,6},{8,7},{9,8},{10,9},{11,1... | collective-permute-start | bytes 2312 | tf_op jit(solution)/shard_map/ppermute | solution.py:28
  10.8 11.0 %collective-permute-start.2 = (s32[12,16]{1,0:T(8,128)S(1)}, s32[12,16]{1,0:T(8,128)S(1)}, u32[]{:S(2)}, u32[]{:S(2)}) collective-permute-start(s32[12,16]{1,0:T(8,128)S(1)} %bitcast.28), channel_id=1, source_target_pairs={{0,2},{1,3},{2,4},{3,5},{4,6},{5,7},{6,8},{7,9},{8,10},{9,11},{10,... | collective-permute-start | bytes 2312 | tf_op jit(solution)/shard_map/ppermute | solution.py:28
  12.7 9.8 %collective-permute-start.3 = (s32[12,16]{1,0:T(8,128)S(1)}, s32[12,16]{1,0:T(8,128)S(1)}, u32[]{:S(2)}, u32[]{:S(2)}) collective-permute-start(s32[12,16]{1,0:T(8,128)S(1)} %bitcast.29), channel_id=1, source_target_pairs={{2,0},{3,1},{4,2},{5,3},{6,4},{7,5},{8,6},{9,7},{10,8},{11,9},{12,... | collective-permute-start | bytes 2312 | tf_op jit(solution)/shard_map/ppermute | solution.py:28
  23.1 25.5 %copy-start.2 = (s32[1,12,16]{2,0,1:T(1,128)S(1)}, s32[1,12,16]{2,0,1:T(1,128)}, u32[]{:S(2)}) copy-start(s32[1,12,16]{2,0,1:T(1,128)} %param.8) | copy-start | bytes 2308
  28.0 27.0 %collective-permute-start.4 = (bf16[2,256,768]{2,1,0:T(8,128)(2,1)}, bf16[2,256,768]{2,1,0:T(8,128)(2,1)S(1)}, u32[]{:S(2)}, u32[]{:S(2)}) collective-permute-start(bf16[2,256,768]{2,1,0:T(8,128)(2,1)} %get-tuple-element.23), channel_id=1, source_target_pairs={{2,0},{3,1},{4,2},{5,3},{6,4},{7,5},{8,6},{9,7},{10,8},{11,9},{12,... | collective-permute-start | bytes 2359304 | tf_op jit(solution)/shard_map/ppermute | solution.py:28
  36.7 38.2 %collective-permute-start.13 = (bf16[2,256,768]{2,1,0:T(8,128)(2,1)}, bf16[2,256,768]{2,1,0:T(8,128)(2,1)}, u32[]{:S(2)}, u32[]{:S(2)}) collective-permute-start(bf16[2,256,768]{2,1,0:T(8,128)(2,1)} %get-tuple-element.32), channel_id=1, source_target_pairs={{1,0},{2,1},{3,2},{4,3},{5,4},{6,5},{7,6},{8,7},{9,8},{10,9},{11,1... | collective-permute-start | bytes 2359304 | tf_op jit(solution)/shard_map/ppermute | solution.py:28
  38.7 38.2 %collective-permute-start.14 = (bf16[2,256,768]{2,1,0:T(8,128)(2,1)}, bf16[2,256,768]{2,1,0:T(8,128)(2,1)}, u32[]{:S(2)}, u32[]{:S(2)}) collective-permute-start(bf16[2,256,768]{2,1,0:T(8,128)(2,1)} %get-tuple-element.33), channel_id=1, source_target_pairs={{0,1},{1,2},{2,3},{3,4},{4,5},{5,6},{6,7},{7,8},{8,9},{9,10},{10,1... | collective-permute-start | bytes 2359304 | tf_op jit(solution)/shard_map/ppermute | solution.py:28
  42.6 46.7 %collective-permute-start.15 = (bf16[2,256,768]{2,1,0:T(8,128)(2,1)}, bf16[2,256,768]{2,1,0:T(8,128)(2,1)}, u32[]{:S(2)}, u32[]{:S(2)}) collective-permute-start(bf16[2,256,768]{2,1,0:T(8,128)(2,1)} %get-tuple-element.34), channel_id=1, source_target_pairs={{0,2},{1,3},{2,4},{3,5},{4,6},{5,7},{6,8},{7,9},{8,10},{9,11},{10,... | collective-permute-start | bytes 2359304 | tf_op jit(solution)/shard_map/ppermute | solution.py:28
  64.2 40.5 %collective-permute-start.10 = (bf16[2,256,512]{2,1,0:T(8,128)(2,1)}, bf16[2,256,512]{2,1,0:T(8,128)(2,1)}, u32[]{:S(2)}, u32[]{:S(2)}) collective-permute-start(bf16[2,256,512]{2,1,0:T(8,128)(2,1)} %get-tuple-element.29), channel_id=1, source_target_pairs={{0,1},{1,2},{2,3},{3,4},{4,5},{5,6},{6,7},{7,8},{8,9},{9,10},{10,1... | collective-permute-start | bytes 1572872 | tf_op jit(solution)/shard_map/ppermute | solution.py:28
  66.1 45.1 %collective-permute-start.11 = (bf16[2,256,512]{2,1,0:T(8,128)(2,1)}, bf16[2,256,512]{2,1,0:T(8,128)(2,1)}, u32[]{:S(2)}, u32[]{:S(2)}) collective-permute-start(bf16[2,256,512]{2,1,0:T(8,128)(2,1)} %get-tuple-element.30), channel_id=1, source_target_pairs={{2,0},{3,1},{4,2},{5,3},{6,4},{7,5},{8,6},{9,7},{10,8},{11,9},{12,... | collective-permute-start | bytes 1572872 | tf_op jit(solution)/shard_map/ppermute | solution.py:28
  75.0 48.0 %collective-permute-start.12 = (bf16[2,256,512]{2,1,0:T(8,128)(2,1)}, bf16[2,256,512]{2,1,0:T(8,128)(2,1)}, u32[]{:S(2)}, u32[]{:S(2)}) collective-permute-start(bf16[2,256,512]{2,1,0:T(8,128)(2,1)} %get-tuple-element.31), channel_id=1, source_target_pairs={{0,2},{1,3},{2,4},{3,5},{4,6},{5,7},{6,8},{7,9},{8,10},{9,11},{10,... | collective-permute-start | bytes 1572872 | tf_op jit(solution)/shard_map/ppermute | solution.py:28
  76.9 48.0 %collective-permute-start.9 = (bf16[2,256,512]{2,1,0:T(8,128)(2,1)}, bf16[2,256,512]{2,1,0:T(8,128)(2,1)}, u32[]{:S(2)}, u32[]{:S(2)}) collective-permute-start(bf16[2,256,512]{2,1,0:T(8,128)(2,1)} %get-tuple-element.28), channel_id=1, source_target_pairs={{1,0},{2,1},{3,2},{4,3},{5,4},{6,5},{7,6},{8,7},{9,8},{10,9},{11,1... | collective-permute-start | bytes 1572872 | tf_op jit(solution)/shard_map/ppermute | solution.py:28
  104.6 74.5 %collective-permute-start.21 = (f32[768,768]{1,0:T(8,128)}, f32[768,768]{1,0:T(8,128)}, u32[]{:S(2)}, u32[]{:S(2)}) collective-permute-start(f32[768,768]{1,0:T(8,128)} %attend_0.1.refs_4_), channel_id=1, source_target_pairs={{0,64},{64,0},{1,65},{65,1},{2,66},{66,2},{3,67},{67,3},{4,68},{68... | collective-permute-start | bytes 7077896 | tf_op jit(solution)/shard_map/ppermute | solution.py:359
  104.7 37.0 %collective-permute-start.17 = (bf16[2,256,768]{2,1,0:T(8,128)(2,1)}, bf16[2,256,768]{2,1,0:T(8,128)(2,1)}, u32[]{:S(2)}, u32[]{:S(2)}) collective-permute-start(bf16[2,256,768]{2,1,0:T(8,128)(2,1)} %get-tuple-element.35), channel_id=1, source_target_pairs={{1,0},{2,1},{3,2},{4,3},{5,4},{6,5},{7,6},{8,7},{9,8},{10,9},{11,1... | collective-permute-start | bytes 2359304 | tf_op jit(solution)/shard_map/ppermute | solution.py:28
  111.3 33.3 %collective-permute-start.18 = (bf16[2,256,768]{2,1,0:T(8,128)(2,1)}, bf16[2,256,768]{2,1,0:T(8,128)(2,1)}, u32[]{:S(2)}, u32[]{:S(2)}) collective-permute-start(bf16[2,256,768]{2,1,0:T(8,128)(2,1)} %get-tuple-element.36), channel_id=1, source_target_pairs={{0,1},{1,2},{2,3},{3,4},{4,5},{5,6},{6,7},{7,8},{8,9},{9,10},{10,1... | collective-permute-start | bytes 2359304 | tf_op jit(solution)/shard_map/ppermute | solution.py:28
  123.0 33.3 %collective-permute-start.19 = (bf16[2,256,768]{2,1,0:T(8,128)(2,1)}, bf16[2,256,768]{2,1,0:T(8,128)(2,1)}, u32[]{:S(2)}, u32[]{:S(2)}) collective-permute-start(bf16[2,256,768]{2,1,0:T(8,128)(2,1)} %get-tuple-element.37), channel_id=1, source_target_pairs={{2,0},{3,1},{4,2},{5,3},{6,4},{7,5},{8,6},{9,7},{10,8},{11,9},{12,... | collective-permute-start | bytes 2359304 | tf_op jit(solution)/shard_map/ppermute | solution.py:28
  124.9 48.7 %collective-permute-start.20 = (bf16[2,256,768]{2,1,0:T(8,128)(2,1)}, bf16[2,256,768]{2,1,0:T(8,128)(2,1)}, u32[]{:S(2)}, u32[]{:S(2)}) collective-permute-start(bf16[2,256,768]{2,1,0:T(8,128)(2,1)} %get-tuple-element.38), channel_id=1, source_target_pairs={{0,2},{1,3},{2,4},{3,5},{4,6},{5,7},{6,8},{7,9},{8,10},{9,11},{10,... | collective-permute-start | bytes 2359304 | tf_op jit(solution)/shard_map/ppermute | solution.py:28
  141.7 53.7 %collective-permute-start.5 = (bf16[2,256,512]{2,1,0:T(8,128)(2,1)}, bf16[2,256,512]{2,1,0:T(8,128)(2,1)}, u32[]{:S(2)}, u32[]{:S(2)}) collective-permute-start(bf16[2,256,512]{2,1,0:T(8,128)(2,1)} %get-tuple-element.24), channel_id=1, source_target_pairs={{1,0},{2,1},{3,2},{4,3},{5,4},{6,5},{7,6},{8,7},{9,8},{10,9},{11,1... | collective-permute-start | bytes 1572872 | tf_op jit(solution)/shard_map/ppermute | solution.py:28
  144.6 50.8 %collective-permute-start.6 = (bf16[2,256,512]{2,1,0:T(8,128)(2,1)}, bf16[2,256,512]{2,1,0:T(8,128)(2,1)}, u32[]{:S(2)}, u32[]{:S(2)}) collective-permute-start(bf16[2,256,512]{2,1,0:T(8,128)(2,1)} %get-tuple-element.25), channel_id=1, source_target_pairs={{0,1},{1,2},{2,3},{3,4},{4,5},{5,6},{6,7},{7,8},{8,9},{9,10},{10,1... | collective-permute-start | bytes 1572872 | tf_op jit(solution)/shard_map/ppermute | solution.py:28
  156.3 39.3 %collective-permute-start.7 = (bf16[2,256,512]{2,1,0:T(8,128)(2,1)}, bf16[2,256,512]{2,1,0:T(8,128)(2,1)}, u32[]{:S(2)}, u32[]{:S(2)}) collective-permute-start(bf16[2,256,512]{2,1,0:T(8,128)(2,1)} %get-tuple-element.26), channel_id=1, source_target_pairs={{2,0},{3,1},{4,2},{5,3},{6,4},{7,5},{8,6},{9,7},{10,8},{11,9},{12,... | collective-permute-start | bytes 1572872 | tf_op jit(solution)/shard_map/ppermute | solution.py:28
  173.6 30.8 %collective-permute-start.8 = (bf16[2,256,512]{2,1,0:T(8,128)(2,1)}, bf16[2,256,512]{2,1,0:T(8,128)(2,1)}, u32[]{:S(2)}, u32[]{:S(2)}) collective-permute-start(bf16[2,256,512]{2,1,0:T(8,128)(2,1)} %get-tuple-element.27), channel_id=1, source_target_pairs={{0,2},{1,3},{2,4},{3,5},{4,6},{5,7},{6,8},{7,9},{8,10},{9,11},{10,... | collective-permute-start | bytes 1572872 | tf_op jit(solution)/shard_map/ppermute | solution.py:28
  179.1 25.3 %collective-permute-start.16 = (f32[768,512]{1,0:T(8,128)}, f32[768,512]{1,0:T(8,128)}, u32[]{:S(2)}, u32[]{:S(2)}) collective-permute-start(f32[768,512]{1,0:T(8,128)} %attend_1.1.refs_5_), channel_id=1, source_target_pairs={{0,64},{64,0},{1,65},{65,1},{2,66},{66,2},{3,67},{67,3},{4,68},{68... | collective-permute-start | bytes 4718600 | tf_op jit(solution)/shard_map/ppermute | solution.py:359
  (5 other events, 3.7 us)

commit v3 on v2

--- a/solution.py
+++ b/solution.py
@@ -11,6 +11,7 @@
 CAP = 4
 GROUP = 4
 REACHES = (1, -1, 2, -2)
+ASKED = (1, 2, -1, -2)
 HANDED = ((0, 6), (6, 4))
 KEPT = ((0, 6), (6, 4))
 guidance_scale = 5.0
@@ -63,7 +64,7 @@
 
 
 def first_pack_kernel(tile, tiles_here, place, order, *refs):
-    listed = refs[: len(REACHES)]
+    listed = [refs[ASKED.index(distance)] for distance in REACHES]
     keys, values = refs[len(REACHES) : len(REACHES) + 2]
     outs = refs[-5 - len(REACHES) : -5]
     picks_out, picks, pools, load_sems, sems = refs[-5:]
@@ -123,92 +124,102 @@
     arrived = refs[: len(REACHES)]
     rest = refs[len(REACHES) :]
     out, q_pool, k_pool, v_pool, scores, tops, result, other_pool, in_sems, out_sems = rest[-10:]
-    width = heads * HD
     rows = tile * tiles_here
-    columns = pl.ds(pl.multiple_of(place[1], HD), width)
-    copies = [pltpu.make_async_copy(queries.at[:, columns], q_pool, in_sems.at[0])]
-    for kind, (own, pool) in enumerate(((keys, k_pool), (values, v_pool))):
-        copies.append(pltpu.make_async_copy(own.at[:, columns], pool.at[pl.ds(0, rows), :], in_sems.at[len(copies)]))
-        for reach in range(len(REACHES)):
-            copies.append(
-                pltpu.make_async_copy(
-                    arrived[reach].at[kind],
-                    pool.at[pl.ds(rows + reach * CAP * tile, CAP * tile), :],
-                    in_sems.at[len(copies)],
-                )
-            )
-    before_scores = 2 + len(REACHES)
+    units = [(first, min(2, heads - first)) for first in range(0, heads, 2)]
     if kept is not None:
-        for piece, (to, source, count) in enumerate(kept[1:]):
-            copies.append(
-                pltpu.make_async_copy(
-                    rest[piece].at[:, pl.ds(source, count)],
-                    other_pool.at[:, pl.ds(to, count)],
-                    in_sems.at[len(copies)],
-                )
-            )
-        out = out.at[:, pl.ds(kept[0], width)]
-    for copy in copies:
-        copy.start()
+        out = out.at[:, pl.ds(kept[0], heads * HD)]
     factor = HD ** (-0.5) * 1.4426950408889634
     side = place[0]
     span = GROUP * tile
     groups = topk // GROUP
     zeros = jnp.zeros((tile, HD), jnp.bfloat16)
+    sems_each = 4 + 2 * len(REACHES)
+
+    def lanes_of(unit):
+        first, count = units[unit]
+        return slice(first * HD, (first + count) * HD)
+
+    loads = []
+    for unit, (first, count) in enumerate(units):
+        here = pl.ds(first * HD, count * HD)
+        own = pl.ds(pl.multiple_of(place[1] + first * HD, HD), count * HD)
+        pairs = [(queries.at[:, own], q_pool.at[:, here])]
+        for kind, (source, pool) in enumerate(((keys, k_pool), (values, v_pool))):
+            pairs.append((source.at[:, own], pool.at[pl.ds(0, rows), here]))
+            for reach in range(len(REACHES)):
+                remote = pl.ds(rows + reach * CAP * tile, CAP * tile)
+                pairs.append((arrived[reach].at[kind, :, here], pool.at[remote, here]))
+        if kept is not None:
+            for piece, (to, source, wide) in enumerate(kept[1:]):
+                start, end = max(to, first * HD), min(to + wide, (first + count) * HD)
+                if start < end:
+                    taken = rest[piece].at[:, pl.ds(source + start - to, end - start)]
+                    pairs.append((taken, other_pool.at[:, pl.ds(start, end - start)]))
+        loads.append(
+            [pltpu.make_async_copy(*pair, in_sems.at[unit * sems_each + i]) for i, pair in enumerate(pairs)]
+        )
+    for copies in loads:
+        for copy in copies:
+            copy.start()
 
     def rows_of(i):
         return pl.ds(pl.multiple_of(i * tile, tile), tile)
 
-    def gathered(pool, i, group, pair):
+    def gathered(pool, i, group, unit):
         picks = [pl.multiple_of(index[i, group * GROUP + j] * tile, tile) for j in range(GROUP)]
-        return jnp.concatenate([pool[pl.ds(p, tile), pair * 2 * HD : (pair + 1) * 2 * HD] for p in picks], axis=0)
-
-    def score(i, slot):
-        for pair in range(heads // 2):
-            lanes = [slice((2 * pair + j) * HD, (2 * pair + j + 1) * HD) for j in range(2)]
-            query = jnp.concatenate(
-                [
-                    jnp.concatenate([q_pool[rows_of(i), lanes[0]], zeros], axis=1),
-                    jnp.concatenate([zeros, q_pool[rows_of(i), lanes[1]]], axis=1),
-                ],
-                axis=0,
-            )
-            top = jnp.full((2 * tile, HD), -jnp.inf, jnp.float32)
+        return jnp.concatenate([pool[pl.ds(p, tile), lanes_of(unit)] for p in picks], axis=0)
+
+    def score(unit, stage):
+        first, count = units[unit]
+        for k in range(2):
+            i = 2 * stage + k
+            query = q_pool[rows_of(i), lanes_of(unit)]
+            if count == 2:
+                query = jnp.concatenate(
+                    [
+                        jnp.concatenate([query[:, :HD], zeros], axis=1),
+                        jnp.concatenate([zeros, query[:, HD:]], axis=1),
+                    ],
+                    axis=0,
+                )
+            top = jnp.full((count * tile, HD), -jnp.inf, jnp.float32)
             for group in range(groups):
                 part = lax.dot_general(
                     query,
-                    gathered(k_pool, i, group, pair),
+                    gathered(k_pool, i, group, unit),
                     (((1,), (1,)), ((), ())),
                     preferred_element_type=jnp.float32,
                 )
                 place_of = lax.broadcasted_iota(jnp.int32, (1, span), 1) + group * span
                 part = jnp.where(place_of < counts[i] * tile, part, -1e30)
-                scores[slot, pair, :, group * span : (group + 1) * span] = part
+                scores[stage % 2, k, : count * tile, group * span : (group + 1) * span] = part
                 for j in range(span // HD):
                     top = jnp.maximum(top, part[:, j * HD : (j + 1) * HD])
-            tops[slot, pair] = jnp.broadcast_to(jnp.max(top, axis=1, keepdims=True), top.shape)
-
-    def mix(i, slot):
-        for pair in range(heads // 2):
-            top = tops[slot, pair]
-            total = jnp.zeros((2 * tile, HD), jnp.float32)
-            mixed = [jnp.zeros((tile, HD), jnp.float32)] * 2
+            tops[stage % 2, k, : count * tile] = jnp.broadcast_to(jnp.max(top, axis=1, keepdims=True), top.shape)
+
+    def mix(unit, stage):
+        first, count = units[unit]
+        for k in range(2):
+            i = 2 * stage + k
+            top = tops[stage % 2, k, : count * tile]
+            total = jnp.zeros((count * tile, HD), jnp.float32)
+            mixed = [jnp.zeros((tile, HD), jnp.float32)] * count
             for group in range(groups):
                 rounded = []
                 for j in range(span // HD):
-                    first = group * span + j * HD
-                    weights = jnp.exp2((scores[slot, pair, :, first : first + HD] - top) * factor)
+                    at = group * span + j * HD
+                    weights = jnp.exp2((scores[stage % 2, k, : count * tile, at : at + HD] - top) * factor)
                     total = total + weights
                     rounded.append(weights.astype(jnp.bfloat16))
                 both = jnp.dot(
                     jnp.concatenate(rounded, axis=1),
-                    gathered(v_pool, i, group, pair),
+                    gathered(v_pool, i, group, unit),
                     preferred_element_type=jnp.float32,
                 )
-                mixed = [mixed[0] + both[:tile, :HD], mixed[1] + both[tile:, HD:]]
+                mixed = [mixed[j] + both[j * tile : (j + 1) * tile, j * HD : (j + 1) * HD] for j in range(count)]
             total = jnp.sum(total, axis=1, keepdims=True)
-            for j in range(2):
-                lanes = slice((2 * pair + j) * HD, (2 * pair + j + 1) * HD)
+            for j in range(count):
+                lanes = slice((first + j) * HD, (first + j + 1) * HD)
                 attended = mixed[j] / total[j * tile : (j + 1) * tile]
                 if kept is not None:
                     other = other_pool[rows_of(i), lanes]
@@ -217,28 +228,50 @@
                     attended = unconditional + guidance_scale * (conditional - unconditional)
                 result[rows_of(i), lanes] = attended
 
-    def copy_out(step):
-        here = pl.ds(pl.multiple_of(step * 2 * tile, 2 * tile), 2 * tile)
-        return pltpu.make_async_copy(result.at[here, :], out.at[here, :], out_sems.at[step])
-
-    for copy in copies[:before_scores]:
+    class Stage:
+        def __init__(self, base, parity):
+            self.base, self.parity = base, parity
+
+        def __rmul__(self, other):
+            return other * (self.base + self.parity)
+
+        def __mod__(self, other):
+            return self.parity
+
+    def copy_out(unit, half):
+        here = pl.ds(half * rows // 2, rows // 2)
+        lanes = pl.ds(units[unit][0] * HD, units[unit][1] * HD)
+        return pltpu.make_async_copy(result.at[here, lanes], out.at[here, lanes], out_sems.at[2 * unit + half])
+
+    stages = tiles_here // 2
+    for copy in loads[0][: 2 + len(REACHES)]:
         copy.wait()
     score(0, 0)
-    for copy in copies[before_scores:]:
-        copy.wait()
-
-    def two_tiles(step, carry):
-        i = step * 2
-        score(i + 1, 1)
-        mix(i, 0)
-        score(jnp.minimum(i + 2, tiles_here - 1), 0)
-        mix(i + 1, 1)
-        copy_out(step).start()
-        return carry
-
-    lax.fori_loop(0, tiles_here // 2, two_tiles, 0)
-    for step in range(tiles_here // 2):
-        copy_out(step).wait()
+    for unit in range(len(units)):
+        for copy in loads[unit][2 + len(REACHES) :]:
+            copy.wait()
+
+        def two_stages(step, carry, unit=unit):
+            base = step * 2
+            score(unit, Stage(base, 1))
+            mix(unit, Stage(base, 0))
+            score(unit, Stage(base + 2, 0))
+            mix(unit, Stage(base, 1))
+            return carry
+
+        lax.fori_loop(0, (stages - 1) // 2, two_stages, 0)
+        copy_out(unit, 0).start()
+        score(unit, stages - 1)
+        mix(unit, stages - 2)
+        if unit + 1 < len(units):
+            for copy in loads[unit + 1][: 2 + len(REACHES)]:
+                copy.wait()
+            score(unit + 1, 0)
+        mix(unit, stages - 1)
+        copy_out(unit, 1).start()
+    for unit in range(len(units)):
+        for half in range(2):
+            copy_out(unit, half).wait()
 
 
 def per_device(queries, keys, values, tile_lists, tile_order):
@@ -299,7 +332,7 @@
 
     counts = jnp.sum((listed >= 0).astype(jnp.int32), axis=1)
 
-    asked = [shifted(listed, "seq", distance) for distance in REACHES]
+    asked = [shifted(listed, "seq", distance) for distance in ASKED]
     *sending, picks = first_pack(asked)
     index = pl.pallas_call(
         functools.partial(index_kernel, tiles_here, devices),
@@ -342,12 +375,12 @@
                 pltpu.VMEM((rows, width), jnp.bfloat16),
                 pltpu.VMEM((pool, width), jnp.bfloat16),
                 pltpu.VMEM((pool, width), jnp.bfloat16),
-                pltpu.VMEM((2, heads // 2, 2 * tile, topk * tile), jnp.float32),
-                pltpu.VMEM((2, heads // 2, 2 * tile, HD), jnp.float32),
+                pltpu.VMEM((2, 2, 2 * tile, topk * tile), jnp.float32),
+                pltpu.VMEM((2, 2, 2 * tile, HD), jnp.float32),
                 pltpu.VMEM((rows, width), jnp.float32),
                 pltpu.VMEM((rows, width) if kept else (8, HD), jnp.float32),
-                pltpu.SemaphoreType.DMA((16,)),
-                pltpu.SemaphoreType.DMA((tiles_here // 2,)),
+                pltpu.SemaphoreType.DMA(((heads + 1) // 2 * (4 + 2 * neighbours),)),
+                pltpu.SemaphoreType.DMA((heads + heads % 2,)),
             ],
             compiler_params=PARAMS,
             cost_estimate=LONG,

time: 218 us -> 213 us (0.977)
  starting transfers between devices: 95.5 us -> 85.1 us
  waiting for transfers between devices: 45.1 us -> 53.8 us
  Pallas kernels: 69.6 us -> 66.7 us
    ppermute x20, starting transfers between devices: 95.3 us -> 85 us  [shifted(): lax.ppermute(value, axis, [(source, source + steps) for source in range(i...]
    ppermute x20, waiting for transfers between devices: 45.1 us -> 53.8 us  [shifted(): lax.ppermute(value, axis, [(source, source + steps) for source in range(i...]
    pallas_call x4, Pallas kernels: 54.8 us -> 51.9 us  [per_device(): pl.pallas_call(functools.partial(attend_kernel, heads, tile, tiles_here,...]
where the time goes in v3:
time: 213 us; the launch traced here: 212 us
  starting transfers between devices  85.1 us (40%)
  Pallas kernels  66.7 us (31%)
  waiting for transfers between devices  53.8 us (25%)
  other arithmetic  3.66 us (2%)
  local copies, waits for them, and re-layouts  2.18 us (1%)
    ppermute x20, starting transfers between devices, shifted(): lax.ppermute(value, axis, [(source, source + steps) for source in range(i...  85 us
    ppermute x20, waiting for transfers between devices, shifted(): lax.ppermute(value, axis, [(source, source + steps) for source in range(i...  53.8 us
    pallas_call x4, Pallas kernels, per_device(): pl.pallas_call(functools.partial(attend_kernel, heads, tile, tiles_here,...  51.9 us
    pallas_call x1, Pallas kernels, later_pack(): pl.pallas_call(functools.partial(later_pack_kernel, tile, len(later)), ou...  8.24 us
    pallas_call x1, Pallas kernels, first_pack(): pl.pallas_call(functools.partial(first_pack_kernel, tile, tiles_here), ou...  4.93 us
  transfers between devices with their start and end apart: 22, of which 9 were waited for; matrix products, arithmetic and copies ran while one was open for 2% of the time, Pallas kernels for 24%

profile of v3, /device:TPU:64, one launch (start us, length us, event | category | flops | bytes accessed | tf_op | source)
XLA Modules:
  0.0 212.0 jit_solution(4836329477568521390)
XLA Ops:
  4.1 4.6 %collective-permute-start.1 = (s32[12,16]{1,0:T(8,128)S(1)}, s32[12,16]{1,0:T(8,128)S(1)}, u32[]{:S(2)}, u32[]{:S(2)}) collective-permute-start(s32[12,16]{1,0:T(8,128)S(1)} %bitcast.27), channel_id=1, source_target_pairs={{0,2},{1,3},{2,4},{3,5},{4,6},{5,7},{6,8},{7,9},{8,10},{9,11},{10,... | collective-permute-start | bytes 2312 | tf_op jit(solution)/shard_map/ppermute | solution.py:29
  8.7 6.4 %collective-permute-start.2 = (s32[12,16]{1,0:T(8,128)S(1)}, s32[12,16]{1,0:T(8,128)S(1)}, u32[]{:S(2)}, u32[]{:S(2)}) collective-permute-start(s32[12,16]{1,0:T(8,128)S(1)} %bitcast.28), channel_id=1, source_target_pairs={{1,0},{2,1},{3,2},{4,3},{5,4},{6,5},{7,6},{8,7},{9,8},{10,9},{11,1... | collective-permute-start | bytes 2312 | tf_op jit(solution)/shard_map/ppermute | solution.py:29
  18.2 4.0 %collective-permute-done.3.refs_3_ = s32[12,16]{1,0:T(8,128)S(1)} collective-permute-done((s32[12,16]{1,0:T(8,128)S(1)}, s32[12,16]{1,0:T(8,128)S(1)}, u32[]{:S(2)}, u32[]{:S(2)}) %collective-permute-start.3) | collective-permute-done | bytes 800 | tf_op jit(solution)/shard_map/ppermute | solution.py:29
  22.7 4.9 %first_pack.1 = (bf16[2,256,768]{2,1,0:T(8,128)(2,1)}, bf16[2,256,768]{2,1,0:T(8,128)(2,1)}, bf16[2,256,768]{2,1,0:T(8,128)(2,1)}, bf16[2,256,768]{2,1,0:T(8,128)(2,1)}, s32[4,8]{1,0:T(4,128)}) custom-call(s32[2]{0:T(128)} %pad_add_fusion.2.place, s32[768]{0:T(1024)} %order.3, s32[12,16]{1,0:T(8,128)} %copy-done.3, s32[12,16]{1,0:T(8,128)} %copy-done.4, ...), custom_call_target="tpu_custom_call" | custom-call | flops 1 | bytes 1 | tf_op jit(solution)/shard_map/first_pack/pallas_call | solution.py:305
  27.7 5.4 %collective-permute-start.4 = (bf16[2,256,768]{2,1,0:T(8,128)(2,1)}, bf16[2,256,768]{2,1,0:T(8,128)(2,1)S(1)}, u32[]{:S(2)}, u32[]{:S(2)}) collective-permute-start(bf16[2,256,768]{2,1,0:T(8,128)(2,1)} %get-tuple-element.23), channel_id=1, source_target_pairs={{2,0},{3,1},{4,2},{5,3},{6,4},{7,5},{8,6},{9,7},{10,8},{11,9},{12,... | collective-permute-start | bytes 2359304 | tf_op jit(solution)/shard_map/ppermute | solution.py:29
  35.1 3.9 %collective-permute-start.14 = (bf16[2,256,768]{2,1,0:T(8,128)(2,1)}, bf16[2,256,768]{2,1,0:T(8,128)(2,1)}, u32[]{:S(2)}, u32[]{:S(2)}) collective-permute-start(bf16[2,256,768]{2,1,0:T(8,128)(2,1)} %get-tuple-element.33), channel_id=1, source_target_pairs={{0,1},{1,2},{2,3},{3,4},{4,5},{5,6},{6,7},{7,8},{8,9},{9,10},{10,1... | collective-permute-start | bytes 2359304 | tf_op jit(solution)/shard_map/ppermute | solution.py:29
  46.0 5.8 %collective-permute-done.4.refs_0_.refs_2_ = bf16[2,256,768]{2,1,0:T(8,128)(2,1)S(1)} collective-permute-done((bf16[2,256,768]{2,1,0:T(8,128)(2,1)}, bf16[2,256,768]{2,1,0:T(8,128)(2,1)S(1)}, u32[]{:S(2)}, u32[]{:S(2)}) %collective-permute-start.4) | collective-permute-done | bytes 786464 | tf_op jit(solution)/shard_map/ppermute | solution.py:29
  52.7 8.2 %later_pack.1 = (bf16[2,256,512]{2,1,0:T(8,128)(2,1)}, bf16[2,256,512]{2,1,0:T(8,128)(2,1)}, bf16[2,256,512]{2,1,0:T(8,128)(2,1)}, bf16[2,256,512]{2,1,0:T(8,128...) custom-call(s32[3]{0:T(128)} %pad_add_fusion.1.place, ...), custom_call_target="tpu_custom_call" | custom-call | flops 1 | bytes 1 | tf_op jit(solution)/shard_map/later_pack/pallas_call | solution.py:318
  62.9 9.4 %collective-permute-start.11 = (bf16[2,256,512]{2,1,0:T(8,128)(2,1)}, bf16[2,256,512]{2,1,0:T(8,128)(2,1)}, u32[]{:S(2)}, u32[]{:S(2)}) collective-permute-start(bf16[2,256,512]{2,1,0:T(8,128)(2,1)} %get-tuple-element.30), channel_id=1, source_target_pairs={{2,0},{3,1},{4,2},{5,3},{6,4},{7,5},{8,6},{9,7},{10,8},{11,9},{12,... | collective-permute-start | bytes 1572872 | tf_op jit(solution)/shard_map/ppermute | solution.py:29
  74.2 7.2 %collective-permute-start.9 = (bf16[2,256,512]{2,1,0:T(8,128)(2,1)}, bf16[2,256,512]{2,1,0:T(8,128)(2,1)}, u32[]{:S(2)}, u32[]{:S(2)}) collective-permute-start(bf16[2,256,512]{2,1,0:T(8,128)(2,1)} %get-tuple-element.28), channel_id=1, source_target_pairs={{1,0},{2,1},{3,2},{4,3},{5,4},{6,5},{7,6},{8,7},{9,8},{10,9},{11,1... | collective-permute-start | bytes 1572872 | tf_op jit(solution)/shard_map/ppermute | solution.py:29
  81.4 4.2 %collective-permute-done.15.refs_3_ = bf16[2,256,768]{2,1,0:T(8,128)(2,1)} collective-permute-done((bf16[2,256,768]{2,1,0:T(8,128)(2,1)}, bf16[2,256,768]{2,1,0:T(8,128)(2,1)}, u32[]{:S(2)}, u32[]{:S(2)}) %collective-permute-start.15) | collective-permute-done | bytes 786464 | tf_op jit(solution)/shard_map/ppermute | solution.py:29
  85.7 14.9 %attend_0.1.refs_4_ = f32[768,768]{1,0:T(8,128)} custom-call(s32[2]{0:T(128)} %pad_add_fusion.5.place, s32[12,16]{1,0:T(8,128)} %pool_index.1.refs_1_.index, s32[12]{0:T(128)} %convert_reduce_fusion.counts, bf16[768,2560]{1,0:T(8,128)(2,1)} %bitcast.31, bf16[768,2560]{1,0:T(8,128)(2,1)} %bitcast.16, bf16[768,2560]{1,0:T(8,128)(2,1)} %bitcast.22, ...), custom_call_target="tpu_custom_call" | custom-call | flops 9999999827968 | bytes 99999997952 | tf_op jit(solution)/shard_map/attend_0/pallas_call | solution.py:368
  103.5 4.7 %collective-permute-done.11.refs_2_ = bf16[2,256,512]{2,1,0:T(8,128)(2,1)} collective-permute-done((bf16[2,256,512]{2,1,0:T(8,128)(2,1)}, bf16[2,256,512]{2,1,0:T(8,128)(2,1)}, u32[]{:S(2)}, u32[]{:S(2)}) %collective-permute-start.11) | collective-permute-done | bytes 524320 | tf_op jit(solution)/shard_map/ppermute | solution.py:29
  110.1 9.3 %collective-permute-done.12.refs_3_ = bf16[2,256,512]{2,1,0:T(8,128)(2,1)} collective-permute-done((bf16[2,256,512]{2,1,0:T(8,128)(2,1)}, bf16[2,256,512]{2,1,0:T(8,128)(2,1)}, u32[]{:S(2)}, u32[]{:S(2)}) %collective-permute-start.12) | collective-permute-done | bytes 524320 | tf_op jit(solution)/shard_map/ppermute | solution.py:29
  122.6 4.4 %collective-permute-start.20 = (bf16[2,256,768]{2,1,0:T(8,128)(2,1)}, bf16[2,256,768]{2,1,0:T(8,128)(2,1)}, u32[]{:S(2)}, u32[]{:S(2)}) collective-permute-start(bf16[2,256,768]{2,1,0:T(8,128)(2,1)} %get-tuple-element.38), channel_id=1, source_target_pairs={{0,2},{1,3},{2,4},{3,5},{4,6},{5,7},{6,8},{7,9},{8,10},{9,11},{10,... | collective-permute-start | bytes 2359304 | tf_op jit(solution)/shard_map/ppermute | solution.py:29
  127.0 11.0 %attend_1.1.refs_5_ = f32[768,512]{1,0:T(8,128)} custom-call(s32[2]{0:T(128)} %pad_add_fusion.3.place, s32[12,16]{1,0:T(8,128)} %pool_index.1.refs_1_.index, s32[12]{0:T(128)} %convert_reduce_fusion.counts, bf16[768,2560]{1,0:T(8,128)(2,1)} %bitcast.32, bf16[768,2560]{1,0:T(8,128)(2,1)} %bitcast.17, bf16[768,2560]{1,0:T(8,128)(2,1)} %bitcast.23, ...), custom_call_target="tpu_custom_call" | custom-call | flops 9999999827968 | bytes 99999997952 | tf_op jit(solution)/shard_map/attend_1/pallas_call | solution.py:368
  138.0 6.1 %collective-permute-start.5 = (bf16[2,256,512]{2,1,0:T(8,128)(2,1)}, bf16[2,256,512]{2,1,0:T(8,128)(2,1)}, u32[]{:S(2)}, u32[]{:S(2)}) collective-permute-start(bf16[2,256,512]{2,1,0:T(8,128)(2,1)} %get-tuple-element.24), channel_id=1, source_target_pairs={{1,0},{2,1},{3,2},{4,3},{5,4},{6,5},{7,6},{8,7},{9,8},{10,9},{11,1... | collective-permute-start | bytes 1572872 | tf_op jit(solution)/shard_map/ppermute | solution.py:29
  146.0 7.2 %collective-permute-done.19.refs_2_ = bf16[2,256,768]{2,1,0:T(8,128)(2,1)} collective-permute-done((bf16[2,256,768]{2,1,0:T(8,128)(2,1)}, bf16[2,256,768]{2,1,0:T(8,128)(2,1)}, u32[]{:S(2)}, u32[]{:S(2)}) %collective-permute-start.19) | collective-permute-done | bytes 786464 | tf_op jit(solution)/shard_map/ppermute | solution.py:29
  153.2 8.5 %collective-permute-start.7 = (bf16[2,256,512]{2,1,0:T(8,128)(2,1)}, bf16[2,256,512]{2,1,0:T(8,128)(2,1)}, u32[]{:S(2)}, u32[]{:S(2)}) collective-permute-start(bf16[2,256,512]{2,1,0:T(8,128)(2,1)} %get-tuple-element.26), channel_id=1, source_target_pairs={{2,0},{3,1},{4,2},{5,3},{6,4},{7,5},{8,6},{9,7},{10,8},{11,9},{12,... | collective-permute-start | bytes 1572872 | tf_op jit(solution)/shard_map/ppermute | solution.py:29
  161.7 8.3 %collective-permute-done.20.refs_3_ = bf16[2,256,768]{2,1,0:T(8,128)(2,1)} collective-permute-done((bf16[2,256,768]{2,1,0:T(8,128)(2,1)}, bf16[2,256,768]{2,1,0:T(8,128)(2,1)}, u32[]{:S(2)}, u32[]{:S(2)}) %collective-permute-start.20) | collective-permute-done | bytes 786464 | tf_op jit(solution)/shard_map/ppermute | solution.py:29
  170.0 5.5 %collective-permute-start.8 = (bf16[2,256,512]{2,1,0:T(8,128)(2,1)}, bf16[2,256,512]{2,1,0:T(8,128)(2,1)}, u32[]{:S(2)}, u32[]{:S(2)}) collective-permute-start(bf16[2,256,512]{2,1,0:T(8,128)(2,1)} %get-tuple-element.27), channel_id=1, source_target_pairs={{0,2},{1,3},{2,4},{3,5},{4,6},{5,7},{6,8},{7,9},{8,10},{9,11},{10,... | collective-permute-start | bytes 1572872 | tf_op jit(solution)/shard_map/ppermute | solution.py:29
  175.6 15.0 %guide_2.1.refs_5_ = f32[768,1280]{1,0:T(8,128)} custom-call(s32[2]{0:T(128)} %get-tuple-element.40.place, s32[12,16]{1,0:T(8,128)} %pool_index.1.refs_1_.index, s32[12]{0:T(128)} %convert_reduce_fusion.counts, bf16[768,2560]{1,0:T(8,128)(2,1)} %bitcast.33, bf16[768,2560]{1,0:T(8,128)(2,1)} %bitcast.18, bf16[768,2560]{1,0:T(8,128)(2,1)} %bitcast.24, ...), custom_call_target="tpu_custom_call" | custom-call | flops 9999999827968 | bytes 99999997952 | tf_op jit(solution)/shard_map/guide_2/pallas_call | solution.py:368
  192.5 8.3 %collective-permute-done.8.refs_3_ = bf16[2,256,512]{2,1,0:T(8,128)(2,1)} collective-permute-done((bf16[2,256,512]{2,1,0:T(8,128)(2,1)}, bf16[2,256,512]{2,1,0:T(8,128)(2,1)}, u32[]{:S(2)}, u32[]{:S(2)}) %collective-permute-start.8) | collective-permute-done | bytes 524320 | tf_op jit(solution)/shard_map/ppermute | solution.py:29
  200.8 11.0 %guide_3.1 = f32[768,1280]{1,0:T(8,128)} custom-call(s32[2]{0:T(128)} %get-tuple-element.39.place, s32[12,16]{1,0:T(8,128)} %pool_index.1.refs_1_.index, s32[12]{0:T(128)} %convert_reduce_fusion.counts, bf16[768,2560]{1,0:T(8,128)(2,1)} %bitcast.34, bf16[768,2560]{1,0:T(8,128)(2,1)} %bitcast.19, ...), custom_call_target="tpu_custom_call", output_to_operand_aliasing={{}: (11, {})} | custom-call | flops 9999999827968 | bytes 99999997952 | tf_op jit(solution)/shard_map/guide_3/pallas_call | solution.py:368
  (48 shorter events, 33.2 us)
Async XLA Ops:
  0.7 27.0 %copy-start.1 = (s32[1,12,16]{2,1,0:T(8,128)}, s32[1,12,16]{2,1,0:T(8,128)S(1)}, u32[]{:S(2)}) copy-start(s32[1,12,16]{2,1,0:T(8,128)S(1)} %copy.11) | copy-start | bytes 2308
  0.7 17.4 %collective-permute-start = (s32[12,16]{1,0:T(8,128)S(1)}, s32[12,16]{1,0:T(8,128)S(1)}, u32[]{:S(2)}, u32[]{:S(2)}) collective-permute-start(s32[12,16]{1,0:T(8,128)S(1)} %bitcast.26), channel_id=1, source_target_pairs={{0,1},{1,2},{2,3},{3,4},{4,5},{5,6},{6,7},{7,8},{8,9},{9,10},{10,1... | collective-permute-start | bytes 2312 | tf_op jit(solution)/shard_map/ppermute | solution.py:29
  4.1 14.0 %collective-permute-start.1 = (s32[12,16]{1,0:T(8,128)S(1)}, s32[12,16]{1,0:T(8,128)S(1)}, u32[]{:S(2)}, u32[]{:S(2)}) collective-permute-start(s32[12,16]{1,0:T(8,128)S(1)} %bitcast.27), channel_id=1, source_target_pairs={{0,2},{1,3},{2,4},{3,5},{4,6},{5,7},{6,8},{7,9},{8,10},{9,11},{10,... | collective-permute-start | bytes 2312 | tf_op jit(solution)/shard_map/ppermute | solution.py:29
  8.7 9.4 %collective-permute-start.2 = (s32[12,16]{1,0:T(8,128)S(1)}, s32[12,16]{1,0:T(8,128)S(1)}, u32[]{:S(2)}, u32[]{:S(2)}) collective-permute-start(s32[12,16]{1,0:T(8,128)S(1)} %bitcast.28), channel_id=1, source_target_pairs={{1,0},{2,1},{3,2},{4,3},{5,4},{6,5},{7,6},{8,7},{9,8},{10,9},{11,1... | collective-permute-start | bytes 2312 | tf_op jit(solution)/shard_map/ppermute | solution.py:29
  15.1 7.0 %collective-permute-start.3 = (s32[12,16]{1,0:T(8,128)S(1)}, s32[12,16]{1,0:T(8,128)S(1)}, u32[]{:S(2)}, u32[]{:S(2)}) collective-permute-start(s32[12,16]{1,0:T(8,128)S(1)} %bitcast.29), channel_id=1, source_target_pairs={{2,0},{3,1},{4,2},{5,3},{6,4},{7,5},{8,6},{9,7},{10,8},{11,9},{12,... | collective-permute-start | bytes 2312 | tf_op jit(solution)/shard_map/ppermute | solution.py:29
  22.7 22.6 %copy-start.2 = (s32[1,12,16]{2,0,1:T(1,128)S(1)}, s32[1,12,16]{2,0,1:T(1,128)}, u32[]{:S(2)}) copy-start(s32[1,12,16]{2,0,1:T(1,128)} %param.8) | copy-start | bytes 2308
  27.7 24.1 %collective-permute-start.4 = (bf16[2,256,768]{2,1,0:T(8,128)(2,1)}, bf16[2,256,768]{2,1,0:T(8,128)(2,1)S(1)}, u32[]{:S(2)}, u32[]{:S(2)}) collective-permute-start(bf16[2,256,768]{2,1,0:T(8,128)(2,1)} %get-tuple-element.23), channel_id=1, source_target_pairs={{2,0},{3,1},{4,2},{5,3},{6,4},{7,5},{8,6},{9,7},{10,8},{11,9},{12,... | collective-permute-start | bytes 2359304 | tf_op jit(solution)/shard_map/ppermute | solution.py:29
  33.1 39.2 %collective-permute-start.13 = (bf16[2,256,768]{2,1,0:T(8,128)(2,1)}, bf16[2,256,768]{2,1,0:T(8,128)(2,1)}, u32[]{:S(2)}, u32[]{:S(2)}) collective-permute-start(bf16[2,256,768]{2,1,0:T(8,128)(2,1)} %get-tuple-element.32), channel_id=1, source_target_pairs={{1,0},{2,1},{3,2},{4,3},{5,4},{6,5},{7,6},{8,7},{9,8},{10,9},{11,1... | collective-permute-start | bytes 2359304 | tf_op jit(solution)/shard_map/ppermute | solution.py:29
  35.1 39.2 %collective-permute-start.14 = (bf16[2,256,768]{2,1,0:T(8,128)(2,1)}, bf16[2,256,768]{2,1,0:T(8,128)(2,1)}, u32[]{:S(2)}, u32[]{:S(2)}) collective-permute-start(bf16[2,256,768]{2,1,0:T(8,128)(2,1)} %get-tuple-element.33), channel_id=1, source_target_pairs={{0,1},{1,2},{2,3},{3,4},{4,5},{5,6},{6,7},{7,8},{8,9},{9,10},{10,1... | collective-permute-start | bytes 2359304 | tf_op jit(solution)/shard_map/ppermute | solution.py:29
  39.0 46.7 %collective-permute-start.15 = (bf16[2,256,768]{2,1,0:T(8,128)(2,1)}, bf16[2,256,768]{2,1,0:T(8,128)(2,1)}, u32[]{:S(2)}, u32[]{:S(2)}) collective-permute-start(bf16[2,256,768]{2,1,0:T(8,128)(2,1)} %get-tuple-element.34), channel_id=1, source_target_pairs={{0,2},{1,3},{2,4},{3,5},{4,6},{5,7},{6,8},{7,9},{8,10},{9,11},{10,... | collective-permute-start | bytes 2359304 | tf_op jit(solution)/shard_map/ppermute | solution.py:29
  61.0 39.7 %collective-permute-start.10 = (bf16[2,256,512]{2,1,0:T(8,128)(2,1)}, bf16[2,256,512]{2,1,0:T(8,128)(2,1)}, u32[]{:S(2)}, u32[]{:S(2)}) collective-permute-start(bf16[2,256,512]{2,1,0:T(8,128)(2,1)} %get-tuple-element.29), channel_id=1, source_target_pairs={{0,1},{1,2},{2,3},{3,4},{4,5},{5,6},{6,7},{7,8},{8,9},{9,10},{10,1... | collective-permute-start | bytes 1572872 | tf_op jit(solution)/shard_map/ppermute | solution.py:29
  62.9 45.3 %collective-permute-start.11 = (bf16[2,256,512]{2,1,0:T(8,128)(2,1)}, bf16[2,256,512]{2,1,0:T(8,128)(2,1)}, u32[]{:S(2)}, u32[]{:S(2)}) collective-permute-start(bf16[2,256,512]{2,1,0:T(8,128)(2,1)} %get-tuple-element.30), channel_id=1, source_target_pairs={{2,0},{3,1},{4,2},{5,3},{6,4},{7,5},{8,6},{9,7},{10,8},{11,9},{12,... | collective-permute-start | bytes 1572872 | tf_op jit(solution)/shard_map/ppermute | solution.py:29
  72.3 47.1 %collective-permute-start.12 = (bf16[2,256,512]{2,1,0:T(8,128)(2,1)}, bf16[2,256,512]{2,1,0:T(8,128)(2,1)}, u32[]{:S(2)}, u32[]{:S(2)}) collective-permute-start(bf16[2,256,512]{2,1,0:T(8,128)(2,1)} %get-tuple-element.31), channel_id=1, source_target_pairs={{0,2},{1,3},{2,4},{3,5},{4,6},{5,7},{6,8},{7,9},{8,10},{9,11},{10,... | collective-permute-start | bytes 1572872 | tf_op jit(solution)/shard_map/ppermute | solution.py:29
  74.2 48.3 %collective-permute-start.9 = (bf16[2,256,512]{2,1,0:T(8,128)(2,1)}, bf16[2,256,512]{2,1,0:T(8,128)(2,1)}, u32[]{:S(2)}, u32[]{:S(2)}) collective-permute-start(bf16[2,256,512]{2,1,0:T(8,128)(2,1)} %get-tuple-element.28), channel_id=1, source_target_pairs={{1,0},{2,1},{3,2},{4,3},{5,4},{6,5},{7,6},{8,7},{9,8},{10,9},{11,1... | collective-permute-start | bytes 1572872 | tf_op jit(solution)/shard_map/ppermute | solution.py:29
  100.6 74.9 %collective-permute-start.21 = (f32[768,768]{1,0:T(8,128)}, f32[768,768]{1,0:T(8,128)}, u32[]{:S(2)}, u32[]{:S(2)}) collective-permute-start(f32[768,768]{1,0:T(8,128)} %attend_0.1.refs_4_), channel_id=1, source_target_pairs={{0,64},{64,0},{1,65},{65,1},{2,66},{66,2},{3,67},{67,3},{4,68},{68... | collective-permute-start | bytes 7077896 | tf_op jit(solution)/shard_map/ppermute | solution.py:392
  100.7 37.3 %collective-permute-start.17 = (bf16[2,256,768]{2,1,0:T(8,128)(2,1)}, bf16[2,256,768]{2,1,0:T(8,128)(2,1)}, u32[]{:S(2)}, u32[]{:S(2)}) collective-permute-start(bf16[2,256,768]{2,1,0:T(8,128)(2,1)} %get-tuple-element.35), channel_id=1, source_target_pairs={{1,0},{2,1},{3,2},{4,3},{5,4},{6,5},{7,6},{8,7},{9,8},{10,9},{11,1... | collective-permute-start | bytes 2359304 | tf_op jit(solution)/shard_map/ppermute | solution.py:29
  108.1 35.9 %collective-permute-start.18 = (bf16[2,256,768]{2,1,0:T(8,128)(2,1)}, bf16[2,256,768]{2,1,0:T(8,128)(2,1)}, u32[]{:S(2)}, u32[]{:S(2)}) collective-permute-start(bf16[2,256,768]{2,1,0:T(8,128)(2,1)} %get-tuple-element.36), channel_id=1, source_target_pairs={{0,1},{1,2},{2,3},{3,4},{4,5},{5,6},{6,7},{7,8},{8,9},{9,10},{10,1... | collective-permute-start | bytes 2359304 | tf_op jit(solution)/shard_map/ppermute | solution.py:29
  119.4 33.8 %collective-permute-start.19 = (bf16[2,256,768]{2,1,0:T(8,128)(2,1)}, bf16[2,256,768]{2,1,0:T(8,128)(2,1)}, u32[]{:S(2)}, u32[]{:S(2)}) collective-permute-start(bf16[2,256,768]{2,1,0:T(8,128)(2,1)} %get-tuple-element.37), channel_id=1, source_target_pairs={{2,0},{3,1},{4,2},{5,3},{6,4},{7,5},{8,6},{9,7},{10,8},{11,9},{12,... | collective-permute-start | bytes 2359304 | tf_op jit(solution)/shard_map/ppermute | solution.py:29
  122.6 47.4 %collective-permute-start.20 = (bf16[2,256,768]{2,1,0:T(8,128)(2,1)}, bf16[2,256,768]{2,1,0:T(8,128)(2,1)}, u32[]{:S(2)}, u32[]{:S(2)}) collective-permute-start(bf16[2,256,768]{2,1,0:T(8,128)(2,1)} %get-tuple-element.38), channel_id=1, source_target_pairs={{0,2},{1,3},{2,4},{3,5},{4,6},{5,7},{6,8},{7,9},{8,10},{9,11},{10,... | collective-permute-start | bytes 2359304 | tf_op jit(solution)/shard_map/ppermute | solution.py:29
  138.0 52.5 %collective-permute-start.5 = (bf16[2,256,512]{2,1,0:T(8,128)(2,1)}, bf16[2,256,512]{2,1,0:T(8,128)(2,1)}, u32[]{:S(2)}, u32[]{:S(2)}) collective-permute-start(bf16[2,256,512]{2,1,0:T(8,128)(2,1)} %get-tuple-element.24), channel_id=1, source_target_pairs={{1,0},{2,1},{3,2},{4,3},{5,4},{6,5},{7,6},{8,7},{9,8},{10,9},{11,1... | collective-permute-start | bytes 1572872 | tf_op jit(solution)/shard_map/ppermute | solution.py:29
  144.1 46.5 %collective-permute-start.6 = (bf16[2,256,512]{2,1,0:T(8,128)(2,1)}, bf16[2,256,512]{2,1,0:T(8,128)(2,1)}, u32[]{:S(2)}, u32[]{:S(2)}) collective-permute-start(bf16[2,256,512]{2,1,0:T(8,128)(2,1)} %get-tuple-element.25), channel_id=1, source_target_pairs={{0,1},{1,2},{2,3},{3,4},{4,5},{5,6},{6,7},{7,8},{8,9},{9,10},{10,1... | collective-permute-start | bytes 1572872 | tf_op jit(solution)/shard_map/ppermute | solution.py:29
  153.2 39.3 %collective-permute-start.7 = (bf16[2,256,512]{2,1,0:T(8,128)(2,1)}, bf16[2,256,512]{2,1,0:T(8,128)(2,1)}, u32[]{:S(2)}, u32[]{:S(2)}) collective-permute-start(bf16[2,256,512]{2,1,0:T(8,128)(2,1)} %get-tuple-element.26), channel_id=1, source_target_pairs={{2,0},{3,1},{4,2},{5,3},{6,4},{7,5},{8,6},{9,7},{10,8},{11,9},{12,... | collective-permute-start | bytes 1572872 | tf_op jit(solution)/shard_map/ppermute | solution.py:29
  170.0 30.8 %collective-permute-start.8 = (bf16[2,256,512]{2,1,0:T(8,128)(2,1)}, bf16[2,256,512]{2,1,0:T(8,128)(2,1)}, u32[]{:S(2)}, u32[]{:S(2)}) collective-permute-start(bf16[2,256,512]{2,1,0:T(8,128)(2,1)} %get-tuple-element.27), channel_id=1, source_target_pairs={{0,2},{1,3},{2,4},{3,5},{4,6},{5,7},{6,8},{7,9},{8,10},{9,11},{10,... | collective-permute-start | bytes 1572872 | tf_op jit(solution)/shard_map/ppermute | solution.py:29
  175.5 25.3 %collective-permute-start.16 = (f32[768,512]{1,0:T(8,128)}, f32[768,512]{1,0:T(8,128)}, u32[]{:S(2)}, u32[]{:S(2)}) collective-permute-start(f32[768,512]{1,0:T(8,128)} %attend_1.1.refs_5_), channel_id=1, source_target_pairs={{0,64},{64,0},{1,65},{65,1},{2,66},{66,2},{3,67},{67,3},{4,68},{68... | collective-permute-start | bytes 4718600 | tf_op jit(solution)/shard_map/ppermute | solution.py:392
  (5 other events, 13.5 us)

commit v4 on v3

--- a/solution.py
+++ b/solution.py
@@ -10,7 +10,7 @@
 HD = 128
 CAP = 4
 GROUP = 4
-REACHES = (1, -1, 2, -2)
+REACHES = (1, 2, -1, -2)
 ASKED = (1, 2, -1, -2)
 HANDED = ((0, 6), (6, 4))
 KEPT = ((0, 6), (6, 4))
@@ -344,7 +344,7 @@
         name="pool_index",
     )(position.astype(jnp.int32)[None], tile_order, listed)
     arrived = [moved(sending)]
-    arrived += [moved(sending) for sending in later_pack(picks, [arrived[0][2], index])]
+    arrived += [moved(sending) for sending in later_pack(picks, [arrived[0][REACHES.index(2)], index])]
     partners, guided, result = [], None, None
     pool = tiles_here * tile + neighbours * CAP * tile
     for chunk, (kept, head, heads, start) in enumerate(chunks):

time: 213 us -> 213 us (level)
  starting transfers between devices: 85.1 us -> 92.9 us
  waiting for transfers between devices: 53.8 us -> 46 us
    ppermute x20, starting transfers between devices: 85 us -> 92.8 us  [shifted(): lax.ppermute(value, axis, [(source, source + steps) for source in range(i...]
    ppermute x20, waiting for transfers between devices: 53.8 us -> 46 us  [shifted(): lax.ppermute(value, axis, [(source, source + steps) for source in range(i...]
where the time goes in v4:
time: 213 us; the launch traced here: 212 us
  starting transfers between devices  92.9 us (44%)
  Pallas kernels  66.7 us (31%)
  waiting for transfers between devices  46 us (22%)
  other arithmetic  3.66 us (2%)
  local copies, waits for them, and re-layouts  2.18 us (1%)
    ppermute x20, starting transfers between devices, shifted(): lax.ppermute(value, axis, [(source, source + steps) for source in range(i...  92.8 us
    pallas_call x4, Pallas kernels, per_device(): pl.pallas_call(functools.partial(attend_kernel, heads, tile, tiles_here,...  51.9 us
    ppermute x20, waiting for transfers between devices, shifted(): lax.ppermute(value, axis, [(source, source + steps) for source in range(i...  46 us
    pallas_call x1, Pallas kernels, later_pack(): pl.pallas_call(functools.partial(later_pack_kernel, tile, len(later)), ou...  8.24 us
    pallas_call x1, Pallas kernels, first_pack(): pl.pallas_call(functools.partial(first_pack_kernel, tile, tiles_here), ou...  4.93 us
  transfers between devices with their start and end apart: 22, of which 9 were waited for; matrix products, arithmetic and copies ran while one was open for 2% of the time, Pallas kernels for 24%

profile of v4, /device:TPU:64, one launch (start us, length us, event | category | flops | bytes accessed | tf_op | source)
XLA Modules:
  0.0 212.0 jit_solution(17605627608349544456)
XLA Ops:
  4.1 4.6 %collective-permute-start.1 = (s32[12,16]{1,0:T(8,128)S(1)}, s32[12,16]{1,0:T(8,128)S(1)}, u32[]{:S(2)}, u32[]{:S(2)}) collective-permute-start(s32[12,16]{1,0:T(8,128)S(1)} %bitcast.27), channel_id=1, source_target_pairs={{0,2},{1,3},{2,4},{3,5},{4,6},{5,7},{6,8},{7,9},{8,10},{9,11},{10,... | collective-permute-start | bytes 2312 | tf_op jit(solution)/shard_map/ppermute | solution.py:29
  8.7 6.4 %collective-permute-start.2 = (s32[12,16]{1,0:T(8,128)S(1)}, s32[12,16]{1,0:T(8,128)S(1)}, u32[]{:S(2)}, u32[]{:S(2)}) collective-permute-start(s32[12,16]{1,0:T(8,128)S(1)} %bitcast.28), channel_id=1, source_target_pairs={{1,0},{2,1},{3,2},{4,3},{5,4},{6,5},{7,6},{8,7},{9,8},{10,9},{11,1... | collective-permute-start | bytes 2312 | tf_op jit(solution)/shard_map/ppermute | solution.py:29
  18.2 4.0 %collective-permute-done.3.refs_3_ = s32[12,16]{1,0:T(8,128)S(1)} collective-permute-done((s32[12,16]{1,0:T(8,128)S(1)}, s32[12,16]{1,0:T(8,128)S(1)}, u32[]{:S(2)}, u32[]{:S(2)}) %collective-permute-start.3) | collective-permute-done | bytes 800 | tf_op jit(solution)/shard_map/ppermute | solution.py:29
  22.7 4.9 %first_pack.1 = (bf16[2,256,768]{2,1,0:T(8,128)(2,1)}, bf16[2,256,768]{2,1,0:T(8,128)(2,1)}, bf16[2,256,768]{2,1,0:T(8,128)(2,1)}, bf16[2,256,768]{2,1,0:T(8,128)(2,1)}, s32[4,8]{1,0:T(4,128)}) custom-call(s32[2]{0:T(128)} %pad_add_fusion.2.place, s32[768]{0:T(1024)} %order.3, s32[12,16]{1,0:T(8,128)} %copy-done.3, s32[12,16]{1,0:T(8,128)} %copy-done.4, ...), custom_call_target="tpu_custom_call" | custom-call | flops 1 | bytes 1 | tf_op jit(solution)/shard_map/first_pack/pallas_call | solution.py:305
  27.7 5.4 %collective-permute-start.4 = (bf16[2,256,768]{2,1,0:T(8,128)(2,1)}, bf16[2,256,768]{2,1,0:T(8,128)(2,1)S(1)}, u32[]{:S(2)}, u32[]{:S(2)}) collective-permute-start(bf16[2,256,768]{2,1,0:T(8,128)(2,1)} %get-tuple-element.23), channel_id=1, source_target_pairs={{2,0},{3,1},{4,2},{5,3},{6,4},{7,5},{8,6},{9,7},{10,8},{11,9},{12,... | collective-permute-start | bytes 2359304 | tf_op jit(solution)/shard_map/ppermute | solution.py:29
  35.1 3.9 %collective-permute-start.14 = (bf16[2,256,768]{2,1,0:T(8,128)(2,1)}, bf16[2,256,768]{2,1,0:T(8,128)(2,1)}, u32[]{:S(2)}, u32[]{:S(2)}) collective-permute-start(bf16[2,256,768]{2,1,0:T(8,128)(2,1)} %get-tuple-element.33), channel_id=1, source_target_pairs={{0,1},{1,2},{2,3},{3,4},{4,5},{5,6},{6,7},{7,8},{8,9},{9,10},{10,1... | collective-permute-start | bytes 2359304 | tf_op jit(solution)/shard_map/ppermute | solution.py:29
  46.0 5.8 %collective-permute-done.4.refs_0_.refs_1_ = bf16[2,256,768]{2,1,0:T(8,128)(2,1)S(1)} collective-permute-done((bf16[2,256,768]{2,1,0:T(8,128)(2,1)}, bf16[2,256,768]{2,1,0:T(8,128)(2,1)S(1)}, u32[]{:S(2)}, u32[]{:S(2)}) %collective-permute-start.4) | collective-permute-done | bytes 786464 | tf_op jit(solution)/shard_map/ppermute | solution.py:29
  52.7 8.2 %later_pack.1 = (bf16[2,256,512]{2,1,0:T(8,128)(2,1)}, bf16[2,256,512]{2,1,0:T(8,128)(2,1)}, bf16[2,256,512]{2,1,0:T(8,128)(2,1)}, bf16[2,256,512]{2,1,0:T(8,128...) custom-call(s32[3]{0:T(128)} %pad_add_fusion.1.place, ...), custom_call_target="tpu_custom_call" | custom-call | flops 1 | bytes 1 | tf_op jit(solution)/shard_map/later_pack/pallas_call | solution.py:318
  61.0 8.4 %collective-permute-start.10 = (bf16[2,256,512]{2,1,0:T(8,128)(2,1)}, bf16[2,256,512]{2,1,0:T(8,128)(2,1)}, u32[]{:S(2)}, u32[]{:S(2)}) collective-permute-start(bf16[2,256,512]{2,1,0:T(8,128)(2,1)} %get-tuple-element.29), channel_id=1, source_target_pairs={{2,0},{3,1},{4,2},{5,3},{6,4},{7,5},{8,6},{9,7},{10,8},{11,9},{12,... | collective-permute-start | bytes 1572872 | tf_op jit(solution)/shard_map/ppermute | solution.py:29
  73.6 7.8 %collective-permute-start.9 = (bf16[2,256,512]{2,1,0:T(8,128)(2,1)}, bf16[2,256,512]{2,1,0:T(8,128)(2,1)}, u32[]{:S(2)}, u32[]{:S(2)}) collective-permute-start(bf16[2,256,512]{2,1,0:T(8,128)(2,1)} %get-tuple-element.28), channel_id=1, source_target_pairs={{1,0},{2,1},{3,2},{4,3},{5,4},{6,5},{7,6},{8,7},{9,8},{10,9},{11,1... | collective-permute-start | bytes 1572872 | tf_op jit(solution)/shard_map/ppermute | solution.py:29
  81.4 4.3 %collective-permute-done.15.refs_3_ = bf16[2,256,768]{2,1,0:T(8,128)(2,1)} collective-permute-done((bf16[2,256,768]{2,1,0:T(8,128)(2,1)}, bf16[2,256,768]{2,1,0:T(8,128)(2,1)}, u32[]{:S(2)}, u32[]{:S(2)}) %collective-permute-start.15) | collective-permute-done | bytes 786464 | tf_op jit(solution)/shard_map/ppermute | solution.py:29
  85.7 14.9 %attend_0.1.refs_4_ = f32[768,768]{1,0:T(8,128)} custom-call(s32[2]{0:T(128)} %pad_add_fusion.5.place, s32[12,16]{1,0:T(8,128)} %pool_index.1.refs_1_.index, s32[12]{0:T(128)} %convert_reduce_fusion.counts, bf16[768,2560]{1,0:T(8,128)(2,1)} %bitcast.31, bf16[768,2560]{1,0:T(8,128)(2,1)} %bitcast.16, bf16[768,2560]{1,0:T(8,128)(2,1)} %bitcast.22, ...), custom_call_target="tpu_custom_call" | custom-call | flops 9999999827968 | bytes 99999997952 | tf_op jit(solution)/shard_map/attend_0/pallas_call | solution.py:368
  100.8 4.1 %collective-permute-start.17 = (bf16[2,256,768]{2,1,0:T(8,128)(2,1)}, bf16[2,256,768]{2,1,0:T(8,128)(2,1)}, u32[]{:S(2)}, u32[]{:S(2)}) collective-permute-start(bf16[2,256,768]{2,1,0:T(8,128)(2,1)} %get-tuple-element.35), channel_id=1, source_target_pairs={{1,0},{2,1},{3,2},{4,3},{5,4},{6,5},{7,6},{8,7},{9,8},{10,9},{11,1... | collective-permute-start | bytes 2359304 | tf_op jit(solution)/shard_map/ppermute | solution.py:29
  111.2 7.7 %collective-permute-done.12.refs_3_ = bf16[2,256,512]{2,1,0:T(8,128)(2,1)} collective-permute-done((bf16[2,256,512]{2,1,0:T(8,128)(2,1)}, bf16[2,256,512]{2,1,0:T(8,128)(2,1)}, u32[]{:S(2)}, u32[]{:S(2)}) %collective-permute-start.12) | collective-permute-done | bytes 524320 | tf_op jit(solution)/shard_map/ppermute | solution.py:29
  120.8 6.2 %collective-permute-start.20 = (bf16[2,256,768]{2,1,0:T(8,128)(2,1)}, bf16[2,256,768]{2,1,0:T(8,128)(2,1)}, u32[]{:S(2)}, u32[]{:S(2)}) collective-permute-start(bf16[2,256,768]{2,1,0:T(8,128)(2,1)} %get-tuple-element.38), channel_id=1, source_target_pairs={{0,2},{1,3},{2,4},{3,5},{4,6},{5,7},{6,8},{7,9},{8,10},{9,11},{10,... | collective-permute-start | bytes 2359304 | tf_op jit(solution)/shard_map/ppermute | solution.py:29
  127.0 11.0 %attend_1.1.refs_5_ = f32[768,512]{1,0:T(8,128)} custom-call(s32[2]{0:T(128)} %pad_add_fusion.3.place, s32[12,16]{1,0:T(8,128)} %pool_index.1.refs_1_.index, s32[12]{0:T(128)} %convert_reduce_fusion.counts, bf16[768,2560]{1,0:T(8,128)(2,1)} %bitcast.32, bf16[768,2560]{1,0:T(8,128)(2,1)} %bitcast.17, bf16[768,2560]{1,0:T(8,128)(2,1)} %bitcast.23, ...), custom_call_target="tpu_custom_call" | custom-call | flops 9999999827968 | bytes 99999997952 | tf_op jit(solution)/shard_map/attend_1/pallas_call | solution.py:368
  138.0 7.5 %collective-permute-start.5 = (bf16[2,256,512]{2,1,0:T(8,128)(2,1)}, bf16[2,256,512]{2,1,0:T(8,128)(2,1)}, u32[]{:S(2)}, u32[]{:S(2)}) collective-permute-start(bf16[2,256,512]{2,1,0:T(8,128)(2,1)} %get-tuple-element.24), channel_id=1, source_target_pairs={{1,0},{2,1},{3,2},{4,3},{5,4},{6,5},{7,6},{8,7},{9,8},{10,9},{11,1... | collective-permute-start | bytes 1572872 | tf_op jit(solution)/shard_map/ppermute | solution.py:29
  147.5 5.1 %collective-permute-done.19.refs_2_ = bf16[2,256,768]{2,1,0:T(8,128)(2,1)} collective-permute-done((bf16[2,256,768]{2,1,0:T(8,128)(2,1)}, bf16[2,256,768]{2,1,0:T(8,128)(2,1)}, u32[]{:S(2)}, u32[]{:S(2)}) %collective-permute-start.19) | collective-permute-done | bytes 786464 | tf_op jit(solution)/shard_map/ppermute | solution.py:29
  152.7 11.2 %collective-permute-start.7 = (bf16[2,256,512]{2,1,0:T(8,128)(2,1)}, bf16[2,256,512]{2,1,0:T(8,128)(2,1)}, u32[]{:S(2)}, u32[]{:S(2)}) collective-permute-start(bf16[2,256,512]{2,1,0:T(8,128)(2,1)} %get-tuple-element.26), channel_id=1, source_target_pairs={{0,1},{1,2},{2,3},{3,4},{4,5},{5,6},{6,7},{7,8},{8,9},{9,10},{10,1... | collective-permute-start | bytes 1572872 | tf_op jit(solution)/shard_map/ppermute | solution.py:29
  163.9 5.7 %collective-permute-done.20.refs_3_ = bf16[2,256,768]{2,1,0:T(8,128)(2,1)} collective-permute-done((bf16[2,256,768]{2,1,0:T(8,128)(2,1)}, bf16[2,256,768]{2,1,0:T(8,128)(2,1)}, u32[]{:S(2)}, u32[]{:S(2)}) %collective-permute-start.20) | collective-permute-done | bytes 786464 | tf_op jit(solution)/shard_map/ppermute | solution.py:29
  169.6 5.9 %collective-permute-start.8 = (bf16[2,256,512]{2,1,0:T(8,128)(2,1)}, bf16[2,256,512]{2,1,0:T(8,128)(2,1)}, u32[]{:S(2)}, u32[]{:S(2)}) collective-permute-start(bf16[2,256,512]{2,1,0:T(8,128)(2,1)} %get-tuple-element.27), channel_id=1, source_target_pairs={{0,2},{1,3},{2,4},{3,5},{4,6},{5,7},{6,8},{7,9},{8,10},{9,11},{10,... | collective-permute-start | bytes 1572872 | tf_op jit(solution)/shard_map/ppermute | solution.py:29
  175.6 15.0 %guide_2.1.refs_5_ = f32[768,1280]{1,0:T(8,128)} custom-call(s32[2]{0:T(128)} %get-tuple-element.40.place, s32[12,16]{1,0:T(8,128)} %pool_index.1.refs_1_.index, s32[12]{0:T(128)} %convert_reduce_fusion.counts, bf16[768,2560]{1,0:T(8,128)(2,1)} %bitcast.33, bf16[768,2560]{1,0:T(8,128)(2,1)} %bitcast.18, bf16[768,2560]{1,0:T(8,128)(2,1)} %bitcast.24, ...), custom_call_target="tpu_custom_call" | custom-call | flops 9999999827968 | bytes 99999997952 | tf_op jit(solution)/shard_map/guide_2/pallas_call | solution.py:368
  192.0 8.8 %collective-permute-done.8.refs_3_ = bf16[2,256,512]{2,1,0:T(8,128)(2,1)} collective-permute-done((bf16[2,256,512]{2,1,0:T(8,128)(2,1)}, bf16[2,256,512]{2,1,0:T(8,128)(2,1)}, u32[]{:S(2)}, u32[]{:S(2)}) %collective-permute-start.8) | collective-permute-done | bytes 524320 | tf_op jit(solution)/shard_map/ppermute | solution.py:29
  200.8 11.0 %guide_3.1 = f32[768,1280]{1,0:T(8,128)} custom-call(s32[2]{0:T(128)} %get-tuple-element.39.place, s32[12,16]{1,0:T(8,128)} %pool_index.1.refs_1_.index, s32[12]{0:T(128)} %convert_reduce_fusion.counts, bf16[768,2560]{1,0:T(8,128)(2,1)} %bitcast.34, bf16[768,2560]{1,0:T(8,128)(2,1)} %bitcast.19, ...), custom_call_target="tpu_custom_call", output_to_operand_aliasing={{}: (11, {})} | custom-call | flops 9999999827968 | bytes 99999997952 | tf_op jit(solution)/shard_map/guide_3/pallas_call | solution.py:368
  (48 shorter events, 33.4 us)
Async XLA Ops:
  0.7 27.0 %copy-start.1 = (s32[1,12,16]{2,1,0:T(8,128)}, s32[1,12,16]{2,1,0:T(8,128)S(1)}, u32[]{:S(2)}) copy-start(s32[1,12,16]{2,1,0:T(8,128)S(1)} %copy.11) | copy-start | bytes 2308
  0.7 17.4 %collective-permute-start = (s32[12,16]{1,0:T(8,128)S(1)}, s32[12,16]{1,0:T(8,128)S(1)}, u32[]{:S(2)}, u32[]{:S(2)}) collective-permute-start(s32[12,16]{1,0:T(8,128)S(1)} %bitcast.26), channel_id=1, source_target_pairs={{0,1},{1,2},{2,3},{3,4},{4,5},{5,6},{6,7},{7,8},{8,9},{9,10},{10,1... | collective-permute-start | bytes 2312 | tf_op jit(solution)/shard_map/ppermute | solution.py:29
  4.1 14.0 %collective-permute-start.1 = (s32[12,16]{1,0:T(8,128)S(1)}, s32[12,16]{1,0:T(8,128)S(1)}, u32[]{:S(2)}, u32[]{:S(2)}) collective-permute-start(s32[12,16]{1,0:T(8,128)S(1)} %bitcast.27), channel_id=1, source_target_pairs={{0,2},{1,3},{2,4},{3,5},{4,6},{5,7},{6,8},{7,9},{8,10},{9,11},{10,... | collective-permute-start | bytes 2312 | tf_op jit(solution)/shard_map/ppermute | solution.py:29
  8.7 9.4 %collective-permute-start.2 = (s32[12,16]{1,0:T(8,128)S(1)}, s32[12,16]{1,0:T(8,128)S(1)}, u32[]{:S(2)}, u32[]{:S(2)}) collective-permute-start(s32[12,16]{1,0:T(8,128)S(1)} %bitcast.28), channel_id=1, source_target_pairs={{1,0},{2,1},{3,2},{4,3},{5,4},{6,5},{7,6},{8,7},{9,8},{10,9},{11,1... | collective-permute-start | bytes 2312 | tf_op jit(solution)/shard_map/ppermute | solution.py:29
  15.1 7.0 %collective-permute-start.3 = (s32[12,16]{1,0:T(8,128)S(1)}, s32[12,16]{1,0:T(8,128)S(1)}, u32[]{:S(2)}, u32[]{:S(2)}) collective-permute-start(s32[12,16]{1,0:T(8,128)S(1)} %bitcast.29), channel_id=1, source_target_pairs={{2,0},{3,1},{4,2},{5,3},{6,4},{7,5},{8,6},{9,7},{10,8},{11,9},{12,... | collective-permute-start | bytes 2312 | tf_op jit(solution)/shard_map/ppermute | solution.py:29
  22.7 22.6 %copy-start.2 = (s32[1,12,16]{2,0,1:T(1,128)S(1)}, s32[1,12,16]{2,0,1:T(1,128)}, u32[]{:S(2)}) copy-start(s32[1,12,16]{2,0,1:T(1,128)} %param.8) | copy-start | bytes 2308
  27.7 24.1 %collective-permute-start.4 = (bf16[2,256,768]{2,1,0:T(8,128)(2,1)}, bf16[2,256,768]{2,1,0:T(8,128)(2,1)S(1)}, u32[]{:S(2)}, u32[]{:S(2)}) collective-permute-start(bf16[2,256,768]{2,1,0:T(8,128)(2,1)} %get-tuple-element.23), channel_id=1, source_target_pairs={{2,0},{3,1},{4,2},{5,3},{6,4},{7,5},{8,6},{9,7},{10,8},{11,9},{12,... | collective-permute-start | bytes 2359304 | tf_op jit(solution)/shard_map/ppermute | solution.py:29
  33.1 38.6 %collective-permute-start.13 = (bf16[2,256,768]{2,1,0:T(8,128)(2,1)}, bf16[2,256,768]{2,1,0:T(8,128)(2,1)}, u32[]{:S(2)}, u32[]{:S(2)}) collective-permute-start(bf16[2,256,768]{2,1,0:T(8,128)(2,1)} %get-tuple-element.32), channel_id=1, source_target_pairs={{1,0},{2,1},{3,2},{4,3},{5,4},{6,5},{7,6},{8,7},{9,8},{10,9},{11,1... | collective-permute-start | bytes 2359304 | tf_op jit(solution)/shard_map/ppermute | solution.py:29
  35.1 38.6 %collective-permute-start.14 = (bf16[2,256,768]{2,1,0:T(8,128)(2,1)}, bf16[2,256,768]{2,1,0:T(8,128)(2,1)}, u32[]{:S(2)}, u32[]{:S(2)}) collective-permute-start(bf16[2,256,768]{2,1,0:T(8,128)(2,1)} %get-tuple-element.33), channel_id=1, source_target_pairs={{0,1},{1,2},{2,3},{3,4},{4,5},{5,6},{6,7},{7,8},{8,9},{9,10},{10,1... | collective-permute-start | bytes 2359304 | tf_op jit(solution)/shard_map/ppermute | solution.py:29
  39.0 46.7 %collective-permute-start.15 = (bf16[2,256,768]{2,1,0:T(8,128)(2,1)}, bf16[2,256,768]{2,1,0:T(8,128)(2,1)}, u32[]{:S(2)}, u32[]{:S(2)}) collective-permute-start(bf16[2,256,768]{2,1,0:T(8,128)(2,1)} %get-tuple-element.34), channel_id=1, source_target_pairs={{0,2},{1,3},{2,4},{3,5},{4,6},{5,7},{6,8},{7,9},{8,10},{9,11},{10,... | collective-permute-start | bytes 2359304 | tf_op jit(solution)/shard_map/ppermute | solution.py:29
  61.0 39.8 %collective-permute-start.10 = (bf16[2,256,512]{2,1,0:T(8,128)(2,1)}, bf16[2,256,512]{2,1,0:T(8,128)(2,1)}, u32[]{:S(2)}, u32[]{:S(2)}) collective-permute-start(bf16[2,256,512]{2,1,0:T(8,128)(2,1)} %get-tuple-element.29), channel_id=1, source_target_pairs={{2,0},{3,1},{4,2},{5,3},{6,4},{7,5},{8,6},{9,7},{10,8},{11,9},{12,... | collective-permute-start | bytes 1572872 | tf_op jit(solution)/shard_map/ppermute | solution.py:29
  69.4 38.7 %collective-permute-start.11 = (bf16[2,256,512]{2,1,0:T(8,128)(2,1)}, bf16[2,256,512]{2,1,0:T(8,128)(2,1)}, u32[]{:S(2)}, u32[]{:S(2)}) collective-permute-start(bf16[2,256,512]{2,1,0:T(8,128)(2,1)} %get-tuple-element.30), channel_id=1, source_target_pairs={{0,1},{1,2},{2,3},{3,4},{4,5},{5,6},{6,7},{7,8},{8,9},{9,10},{10,1... | collective-permute-start | bytes 1572872 | tf_op jit(solution)/shard_map/ppermute | solution.py:29
  71.7 47.2 %collective-permute-start.12 = (bf16[2,256,512]{2,1,0:T(8,128)(2,1)}, bf16[2,256,512]{2,1,0:T(8,128)(2,1)}, u32[]{:S(2)}, u32[]{:S(2)}) collective-permute-start(bf16[2,256,512]{2,1,0:T(8,128)(2,1)} %get-tuple-element.31), channel_id=1, source_target_pairs={{0,2},{1,3},{2,4},{3,5},{4,6},{5,7},{6,8},{7,9},{8,10},{9,11},{10,... | collective-permute-start | bytes 1572872 | tf_op jit(solution)/shard_map/ppermute | solution.py:29
  73.6 47.2 %collective-permute-start.9 = (bf16[2,256,512]{2,1,0:T(8,128)(2,1)}, bf16[2,256,512]{2,1,0:T(8,128)(2,1)}, u32[]{:S(2)}, u32[]{:S(2)}) collective-permute-start(bf16[2,256,512]{2,1,0:T(8,128)(2,1)} %get-tuple-element.28), channel_id=1, source_target_pairs={{1,0},{2,1},{3,2},{4,3},{5,4},{6,5},{7,6},{8,7},{9,8},{10,9},{11,1... | collective-permute-start | bytes 1572872 | tf_op jit(solution)/shard_map/ppermute | solution.py:29
  100.7 74.9 %collective-permute-start.21 = (f32[768,768]{1,0:T(8,128)}, f32[768,768]{1,0:T(8,128)}, u32[]{:S(2)}, u32[]{:S(2)}) collective-permute-start(f32[768,768]{1,0:T(8,128)} %attend_0.1.refs_4_), channel_id=1, source_target_pairs={{0,64},{64,0},{1,65},{65,1},{2,66},{66,2},{3,67},{67,3},{4,68},{68... | collective-permute-start | bytes 7077896 | tf_op jit(solution)/shard_map/ppermute | solution.py:392
  100.8 37.3 %collective-permute-start.17 = (bf16[2,256,768]{2,1,0:T(8,128)(2,1)}, bf16[2,256,768]{2,1,0:T(8,128)(2,1)}, u32[]{:S(2)}, u32[]{:S(2)}) collective-permute-start(bf16[2,256,768]{2,1,0:T(8,128)(2,1)} %get-tuple-element.35), channel_id=1, source_target_pairs={{1,0},{2,1},{3,2},{4,3},{5,4},{6,5},{7,6},{8,7},{9,8},{10,9},{11,1... | collective-permute-start | bytes 2359304 | tf_op jit(solution)/shard_map/ppermute | solution.py:29
  108.1 37.5 %collective-permute-start.18 = (bf16[2,256,768]{2,1,0:T(8,128)(2,1)}, bf16[2,256,768]{2,1,0:T(8,128)(2,1)}, u32[]{:S(2)}, u32[]{:S(2)}) collective-permute-start(bf16[2,256,768]{2,1,0:T(8,128)(2,1)} %get-tuple-element.36), channel_id=1, source_target_pairs={{2,0},{3,1},{4,2},{5,3},{6,4},{7,5},{8,6},{9,7},{10,8},{11,9},{12,... | collective-permute-start | bytes 2359304 | tf_op jit(solution)/shard_map/ppermute | solution.py:29
  118.9 33.7 %collective-permute-start.19 = (bf16[2,256,768]{2,1,0:T(8,128)(2,1)}, bf16[2,256,768]{2,1,0:T(8,128)(2,1)}, u32[]{:S(2)}, u32[]{:S(2)}) collective-permute-start(bf16[2,256,768]{2,1,0:T(8,128)(2,1)} %get-tuple-element.37), channel_id=1, source_target_pairs={{0,1},{1,2},{2,3},{3,4},{4,5},{5,6},{6,7},{7,8},{8,9},{9,10},{10,1... | collective-permute-start | bytes 2359304 | tf_op jit(solution)/shard_map/ppermute | solution.py:29
  120.8 48.7 %collective-permute-start.20 = (bf16[2,256,768]{2,1,0:T(8,128)(2,1)}, bf16[2,256,768]{2,1,0:T(8,128)(2,1)}, u32[]{:S(2)}, u32[]{:S(2)}) collective-permute-start(bf16[2,256,768]{2,1,0:T(8,128)(2,1)} %get-tuple-element.38), channel_id=1, source_target_pairs={{0,2},{1,3},{2,4},{3,5},{4,6},{5,7},{6,8},{7,9},{8,10},{9,11},{10,... | collective-permute-start | bytes 2359304 | tf_op jit(solution)/shard_map/ppermute | solution.py:29
  138.0 52.5 %collective-permute-start.5 = (bf16[2,256,512]{2,1,0:T(8,128)(2,1)}, bf16[2,256,512]{2,1,0:T(8,128)(2,1)}, u32[]{:S(2)}, u32[]{:S(2)}) collective-permute-start(bf16[2,256,512]{2,1,0:T(8,128)(2,1)} %get-tuple-element.24), channel_id=1, source_target_pairs={{1,0},{2,1},{3,2},{4,3},{5,4},{6,5},{7,6},{8,7},{9,8},{10,9},{11,1... | collective-permute-start | bytes 1572872 | tf_op jit(solution)/shard_map/ppermute | solution.py:29
  145.6 45.0 %collective-permute-start.6 = (bf16[2,256,512]{2,1,0:T(8,128)(2,1)}, bf16[2,256,512]{2,1,0:T(8,128)(2,1)}, u32[]{:S(2)}, u32[]{:S(2)}) collective-permute-start(bf16[2,256,512]{2,1,0:T(8,128)(2,1)} %get-tuple-element.25), channel_id=1, source_target_pairs={{2,0},{3,1},{4,2},{5,3},{6,4},{7,5},{8,6},{9,7},{10,8},{11,9},{12,... | collective-permute-start | bytes 1572872 | tf_op jit(solution)/shard_map/ppermute | solution.py:29
  152.7 39.4 %collective-permute-start.7 = (bf16[2,256,512]{2,1,0:T(8,128)(2,1)}, bf16[2,256,512]{2,1,0:T(8,128)(2,1)}, u32[]{:S(2)}, u32[]{:S(2)}) collective-permute-start(bf16[2,256,512]{2,1,0:T(8,128)(2,1)} %get-tuple-element.26), channel_id=1, source_target_pairs={{0,1},{1,2},{2,3},{3,4},{4,5},{5,6},{6,7},{7,8},{8,9},{9,10},{10,1... | collective-permute-start | bytes 1572872 | tf_op jit(solution)/shard_map/ppermute | solution.py:29
  169.6 31.3 %collective-permute-start.8 = (bf16[2,256,512]{2,1,0:T(8,128)(2,1)}, bf16[2,256,512]{2,1,0:T(8,128)(2,1)}, u32[]{:S(2)}, u32[]{:S(2)}) collective-permute-start(bf16[2,256,512]{2,1,0:T(8,128)(2,1)} %get-tuple-element.27), channel_id=1, source_target_pairs={{0,2},{1,3},{2,4},{3,5},{4,6},{5,7},{6,8},{7,9},{8,10},{9,11},{10,... | collective-permute-start | bytes 1572872 | tf_op jit(solution)/shard_map/ppermute | solution.py:29
  175.5 25.3 %collective-permute-start.16 = (f32[768,512]{1,0:T(8,128)}, f32[768,512]{1,0:T(8,128)}, u32[]{:S(2)}, u32[]{:S(2)}) collective-permute-start(f32[768,512]{1,0:T(8,128)} %attend_1.1.refs_5_), channel_id=1, source_target_pairs={{0,64},{64,0},{1,65},{65,1},{2,66},{66,2},{3,67},{67,3},{4,68},{68... | collective-permute-start | bytes 4718600 | tf_op jit(solution)/shard_map/ppermute | solution.py:392
  (5 other events, 13.5 us)
